TPU v7x, 256 devices: a whole 4x4x8 slice. The times are simulated.
256 devices in a mesh: dp: 32 (over y, x, core), tensor: 8 (over z).
Axes of the slice: x: 4, y: 4, z: 8, core: 2. Of those that a mesh axis runs over, the one named last changes fastest.
Arguments:
- patches: bfloat16 [65536, 1280], P('dp', 'tensor'), may hold values from -6 to 6
- norm_gain: bfloat16 [1280], P('tensor'), may hold values from 0.5 to 1.5
- w_first: bfloat16 [2560, 4, 1280], P('dp', None, 'tensor'), may hold values from -0.078125 to 0.078125
- b_first: bfloat16 [2560], P('tensor'), may hold values from -3 to 3
- w_second: bfloat16 [4096, 2560], P('dp', 'tensor'), may hold values from -0.125 to 0.125
- b_second: bfloat16 [4096], P('tensor'), may hold values from -3 to 3
- counts: int32 [32], replicated, may hold values from 1 to 32, 512 in all
- cotangent: bfloat16 [16384, 4096], P('dp', 'tensor'), may hold values from -0.0625 to 0.0625
Outputs:
- embeddings: bfloat16 [16384, 4096], P('dp', 'tensor')
- grad_w1: bfloat16 [2560, 4, 1280], P('dp', None, 'tensor')
- grad_w2: bfloat16 [4096, 2560], P('dp', 'tensor')
Inputs may be any that keep to these rules, and one draw needn't show every extreme that they name: counts sum to 512 and one rank holds exactly 32 live windows; live windows occupy a rank's first slots.
All inputs are finite; a program needn't handle non-finite values.
Results may differ from a plain program's by a relative error of at most 0.028.
Values may be sent and summed in bfloat16 or wider, within the bound.
A program may use at most 64 MiB of HBM per device.

v0:
```python
import jax
import jax.numpy as jnp
from jax import lax
from jax.sharding import PartitionSpec as P

D = 1280
PATCH = 64
WIN = 16


def gelu_parts(values):
    normal_cdf = 0.5 * (1.0 + lax.erf(values * 0.7071067811865476))
    density = jnp.exp(-0.5 * values * values) * 0.3989422804014327
    return (values * normal_cdf, normal_cdf + values * density)


def pick_rows(source, indices, keep_mask):
    taken = jnp.take(source, indices, axis=0)
    shape_mask = keep_mask.reshape(keep_mask.shape + (1,) * (taken.ndim - 1))
    return jnp.where(shape_mask, taken, jnp.zeros_like(taken))


def on_device(patches, norm_gain, w_first, b_first, w_second, b_second, counts, cotangent):
    dp_size = lax.axis_size("dp")
    rank_here = lax.axis_index("dp")
    own_slots = patches.shape[0] // PATCH
    feat_width = patches.shape[1]
    out_width = cotangent.shape[1]
    per_peer = (own_slots + dp_size - 1) // dp_size
    tokens_here = WIN * PATCH // 4
    ends = jnp.cumsum(counts)
    starts = ends - counts
    mine_start = starts[rank_here]
    mine_count = counts[rank_here]
    targets = jnp.arange(dp_size, dtype=jnp.int32)[:, None]
    rounds = jnp.arange(per_peer, dtype=jnp.int32)[None, :]
    send_slot = rounds * dp_size + jnp.remainder(targets - mine_start, dp_size)
    send_live = (send_slot < mine_count).reshape(-1)
    send_slot = jnp.minimum(send_slot, own_slots - 1).reshape(-1)
    compute_slot = jnp.arange(WIN, dtype=jnp.int32)
    global_pos = compute_slot * dp_size + rank_here
    sources = jnp.sum((ends[None, :] <= global_pos[:, None]).astype(jnp.int32), axis=1)
    recv_index = sources * per_peer + (global_pos - starts[sources]) // dp_size
    back_slot = rounds * dp_size + jnp.remainder(rank_here - starts[:, None], dp_size)
    back_live = (back_slot < counts[:, None]).reshape(-1)
    back_slot = jnp.minimum((starts[:, None] + back_slot) // dp_size, WIN - 1).reshape(-1)
    home_slot = jnp.arange(own_slots, dtype=jnp.int32)
    home_index = jnp.remainder(mine_start + home_slot, dp_size) * per_peer + home_slot // dp_size
    home_live = home_slot < mine_count
    windows = patches.reshape(own_slots, PATCH, feat_width)
    outgoing = pick_rows(windows, send_slot, send_live).reshape(
        dp_size, per_peer, PATCH, feat_width
    )
    inbound = lax.all_to_all(outgoing, "dp", split_axis=0, concat_axis=0, tiled=True)
    gathered_rows = jnp.take(
        inbound.reshape(dp_size * per_peer, PATCH, feat_width), recv_index, axis=0
    )
    floats = gathered_rows.reshape(WIN * PATCH, feat_width).astype(jnp.float32)
    squares = lax.psum(jnp.sum(floats * floats, axis=1), "tensor")
    normed = (
        floats * lax.rsqrt(squares / D + 1e-06)[:, None] * norm_gain.astype(jnp.float32)
    ).astype(jnp.bfloat16)
    merged = normed.reshape(tokens_here, 4 * feat_width)
    piece = lax.all_gather(w_first, "dp", axis=0, tiled=True)
    flat_piece = piece.reshape(piece.shape[0], 4 * feat_width)
    partial_hidden = lax.dot_general(
        merged, flat_piece, (((1,), (1,)), ((), ())), preferred_element_type=jnp.float32
    )
    pre_act = lax.psum_scatter(
        partial_hidden.astype(jnp.bfloat16), "tensor", scatter_dimension=1, tiled=True
    ).astype(jnp.float32) + b_first.astype(jnp.float32)
    activated, slopes = gelu_parts(pre_act)
    hidden = activated.astype(jnp.bfloat16)
    partial_embed = lax.dot_general(
        hidden,
        lax.all_gather(w_second, "dp", axis=0, tiled=True),
        (((1,), (1,)), ((), ())),
        preferred_element_type=jnp.float32,
    )
    embed = lax.psum_scatter(
        partial_embed.astype(jnp.bfloat16), "tensor", scatter_dimension=1, tiled=True
    ).astype(jnp.float32) + b_second.astype(jnp.float32)
    embed = embed.astype(jnp.bfloat16).reshape(WIN, PATCH // 4, out_width)
    going_home = pick_rows(embed, back_slot, back_live).reshape(
        dp_size, per_peer, PATCH // 4, out_width
    )
    arrived = lax.all_to_all(going_home, "dp", split_axis=0, concat_axis=0, tiled=True)
    arrived = arrived.reshape(dp_size * per_peer, PATCH // 4, out_width)
    embeddings = pick_rows(arrived, home_index, home_live).reshape(
        own_slots * PATCH // 4, out_width
    )
    cot_windows = cotangent.reshape(own_slots, PATCH // 4, out_width)
    cot_outgoing = pick_rows(cot_windows, send_slot, send_live).reshape(
        dp_size, per_peer, PATCH // 4, out_width
    )
    grad_inbound = lax.all_to_all(cot_outgoing, "dp", split_axis=0, concat_axis=0, tiled=True)
    grad_local = jnp.take(
        grad_inbound.reshape(dp_size * per_peer, PATCH // 4, out_width), recv_index, axis=0
    )
    grad_full = lax.all_gather(
        grad_local.reshape(tokens_here, out_width), "tensor", axis=1, tiled=True
    )
    columns = grad_full
    grad_w2 = lax.psum_scatter(
        lax.dot_general(
            columns, hidden, (((0,), (0,)), ((), ())), preferred_element_type=jnp.float32
        ).astype(jnp.bfloat16),
        "dp",
        scatter_dimension=0,
        tiled=True,
    )
    columns = grad_full
    grad_hidden = jnp.dot(
        columns,
        lax.all_gather(w_second, "dp", axis=0, tiled=True),
        preferred_element_type=jnp.float32,
    )
    grad_pre = (grad_hidden * slopes).astype(jnp.bfloat16)
    grad_pre_full = lax.all_gather(grad_pre, "tensor", axis=1, tiled=True)
    columns = grad_pre_full
    grad_w1 = lax.psum_scatter(
        lax.dot_general(
            columns, merged, (((0,), (0,)), ((), ())), preferred_element_type=jnp.float32
        ).astype(jnp.bfloat16),
        "dp",
        scatter_dimension=0,
        tiled=True,
    ).astype(jnp.float32)
    grad_w1 = grad_w1.reshape(w_first.shape).astype(jnp.bfloat16)
    return (embeddings, grad_w1, grad_w2)


def solution(mesh):
    in_specs = (
        P("dp", "tensor"),
        P("tensor"),
        P("dp", None, "tensor"),
        P("tensor"),
        P("dp", "tensor"),
        P("tensor"),
        P(),
        P("dp", "tensor"),
    )
    out_specs = (P("dp", "tensor"), P("dp", None, "tensor"), P("dp", "tensor"))
    return jax.shard_map(
        on_device, mesh=mesh, in_specs=in_specs, out_specs=out_specs, check_vma=False
    )
```

profile of v0, /device:TPU:164, one launch (start us, length us, event | category | flops | bytes accessed | tf_op | source)
XLA Modules:
  0.0 485.5 jit_solution(18138270178006651806)
XLA Ops:
  7.2 1.6 copy.44
  8.9 0.8 copy.39
  9.7 0.1 reduce-window.8
  9.8 0.1 reduce.1
  9.9 1.3 dynamic_slice.6
  11.2 0.7 fusion.31
  11.8 0.6 dynamic_slice.7
  12.4 0.7 compare_select_fusion.3
  13.1 0.6 gather_fusion.6
  13.7 1.3 compare_and_fusion.1
  15.0 0.9 fusion.5
  15.9 7.6 %all-to-all-start.2 = ((bf16[32,1,16,512]{3,2,1,0:T(8,128)(2,1)}), bf16[32,1,16,512]{3,2,1,0:T(8,128)(2,1)S(1)}, u32[]{:S(2)}, u32[]{:S(2)}) async-start(bf16[32,1,16,512]{3,2,1,0:T(8,128)(2,1)} %fusion.5), calls=%async_computation.4 | async-start | bytes 1048576 | tf_op jit(solution)/shard_map/all_to_all | solution.py:96
  23.5 0.0 all-gather.9.cloned.1.call-start
  23.6 0.2 convert_reduce_fusion
  23.8 0.7 gather_fusion
  24.5 0.1 broadcast_in_dim.104
  24.5 0.1 broadcast_in_dim.105
  24.7 9.5 %all-to-all-done.2 = bf16[32,1,16,512]{3,2,1,0:T(8,128)(2,1)S(1)} async-done(((bf16[32,1,16,512]{3,2,1,0:T(8,128)(2,1)}), bf16[32,1,16,512]{3,2,1,0:T(8,128)(2,1)S(1)}, u32[]{:S(2)}, u32[]{:S(2)}) %all-to-all-start.2) | async-done | bytes 524320 | tf_op jit(solution)/shard_map/all_to_all | solution.py:96
  34.2 0.6 gather_fusion.4
  34.7 0.8 bitcast_select_fusion.2
  35.6 0.7 all-gather.7.cloned.1.call-update
  36.3 0.5 copy.47
  36.8 0.7 fusion.26
  37.5 0.6 gather_fusion.1
  38.1 1.2 fusion.3
  39.3 6.3 %all-to-all-start = ((bf16[32,1,64,160]{3,2,1,0:T(8,128)(2,1)}), bf16[32,1,64,160]{3,2,1,0:T(8,128)(2,1)S(1)}, u32[]{:S(2)}, u32[]{:S(2)}) async-start(bf16[32,1,64,160]{3,2,1,0:T(8,128)(2,1)} %fusion.3), calls=%async_computation | async-start | bytes 2097152 | tf_op jit(solution)/shard_map/all_to_all | solution.py:54
  45.7 0.0 reduce-scatter.7.cloned.1.call-start
  45.7 19.6 %all-to-all-done = bf16[32,1,64,160]{3,2,1,0:T(8,128)(2,1)S(1)} async-done(((bf16[32,1,64,160]{3,2,1,0:T(8,128)(2,1)}), bf16[32,1,64,160]{3,2,1,0:T(8,128)(2,1)S(1)}, u32[]{:S(2)}, u32[]{:S(2)}) %all-to-all-start) | async-done | bytes 655392 | tf_op jit(solution)/shard_map/all_to_all | solution.py:54
  65.4 0.6 gather_fusion.2
  66.0 0.2 gather.39
  66.1 0.3 multiply_reduce_fusion
  66.4 0.1 reduce_sum.25
  66.5 14.8 %psum.7 = f32[1024]{0:T(1024)S(1)} all-reduce(f32[1024]{0:T(1024)S(1)} %reduce_sum.25), channel_id=1, replica_groups=mesh['dp'=32,'tensor'=8] {'tensor'}, use_global_device_ids=true, to_apply=%region_3.4 | all-reduce | flops 1024 | bytes 8192 | tf_op jit(solution)/shard_map/psum | solution.py:59
  81.3 0.1 mul.94
  81.5 0.1 copy.43
  81.5 0.3 copy.42
  81.9 4.9 %fusion = bf16[256,2560]{0,1:T(8,128)(2,1)} fusion(bf16[2560,4,160]{2,0,1:T(8,128)(2,1)} %all-gather.5.cloned.1.call-done, f32[160]{0:T(256)S(1)} %convert_element_type.64, f32[256,4]{0,1:T(4,128)S(1)} %copy.43, bf16[256,4,160]{0,2,1:T(8,128)(2,1)S(1)} %copy.42, pred[256]{0:T(512)(128)(4,1)S(1)} %broadcast_in_dim.105), kind=kOutput, calls=%fused_computation.11 | convolution fusion | flops 840335360 | bytes 4920192 | tf_op jit(solution)/shard_map/dot_general | solution.py:66
  87.0 26.8 %all-gather.9.cloned.1.call-done = bf16[256,4096]{1,0:T(8,128)(2,1)} async-done(((bf16[256,512]{1,0:T(8,128)(2,1)}), bf16[256,4096]{1,0:T(8,128)(2,1)}) %all-gather.9.cloned.1.call-update) | async-done | bytes 2097168 | tf_op jit(solution)/shard_map/all_gather | solution.py:100
  113.7 52.6 %all-gather.7.cloned.1.call-done = bf16[4096,320]{0,1:T(8,128)(2,1)} async-done(((bf16[128,320]{0,1:T(8,128)(2,1)}), bf16[4096,320]{0,1:T(8,128)(2,1)}) %all-gather.7.cloned.1.call-update) | async-done | bytes 2621456 | tf_op jit(solution)/shard_map/all_gather | solution.py:76
  166.3 40.8 %reduce-scatter.7.cloned.1.call-done = bf16[256,320]{0,1:T(8,128)(2,1)} async-done(((bf16[256,2560]{0,1:T(8,128)(2,1)}), bf16[256,320]{0,1:T(8,128)(2,1)}) %reduce-scatter.7.cloned.1.call-update) | async-done | bytes 163856 | tf_op jit(solution)/shard_map/reduce_scatter | solution.py:69
  207.2 4.0 fusion.1
  211.2 2.7 convolution_convert_fusion.1
  214.0 2.5 convolution_convert_fusion
  216.5 2.8 copy.48
  219.5 0.1 mul.114
  219.5 0.9 copy-done.2
  220.4 0.7 gather.44
  221.1 0.2 copy.46
  221.4 27.8 %all-gather.11.cloned.1.call-done = bf16[256,2560]{0,1:T(8,128)(2,1)} async-done(((bf16[256,320]{0,1:T(8,128)(2,1)}), bf16[256,2560]{0,1:T(8,128)(2,1)}) %all-gather.11.cloned.1.call-update) | async-done | bytes 1310736 | tf_op jit(solution)/shard_map/all_gather | solution.py:119
  249.1 4.3 convolution_convert_fusion.2
  253.5 0.7 copy-done.7
  254.2 38.4 %reduce-scatter.9.cloned.1.call-done = bf16[256,512]{1,0:T(8,128)(2,1)} async-done(((bf16[256,4096]{1,0:T(8,128)(2,1)}), bf16[256,512]{1,0:T(8,128)(2,1)}) %reduce-scatter.9.cloned.1.call-update) | async-done | bytes 262160 | tf_op jit(solution)/shard_map/reduce_scatter | solution.py:80
  292.6 1.0 add_convert_fusion
  293.6 0.6 gather_fusion.3
  294.2 0.9 fusion.4
  295.1 7.2 %all-to-all-start.1 = ((bf16[32,1,16,512]{3,2,1,0:T(8,128)(2,1)}), bf16[32,1,16,512]{3,2,1,0:T(8,128)(2,1)S(1)}, u32[]{:S(2)}, u32[]{:S(2)}) async-start(bf16[32,1,16,512]{3,2,1,0:T(8,128)(2,1)} %fusion.4), calls=%async_computation.3 | async-start | bytes 1048576 | tf_op jit(solution)/shard_map/all_to_all | solution.py:87
  302.3 0.7 compare_select_fusion
  302.9 1.3 compare_and_fusion
  304.2 80.5 %reduce-scatter.13.cloned.1.call-done = bf16[128,320]{1,0:T(8,128)(2,1)} async-done(((bf16[4096,320]{1,0:T(8,128)(2,1)}), bf16[128,320]{1,0:T(8,128)(2,1)}) %reduce-scatter.13.cloned.1.call-update) | async-done | bytes 81936
  384.7 1.6 copy.49
  386.3 0.6 gather_fusion.5
  386.9 0.9 select_select_fusion.1
  387.9 89.1 %reduce-scatter.11.cloned.1.call-done = bf16[80,640]{1,0:T(8,128)(2,1)} async-done(((bf16[2560,640]{1,0:T(8,128)(2,1)}), bf16[80,640]{1,0:T(8,128)(2,1)}) %reduce-scatter.11.cloned.1.call-update) | async-done | bytes 102416 | tf_op jit(solution)/shard_map/reduce_scatter | solution.py:121
  477.0 1.7 convert_element_type.78
  (48 shorter events, 0.6 us)
Async XLA Ops:
  7.2 5.9 %copy-start = (bf16[512,512]{1,0:T(8,128)(2,1)S(1)}, bf16[512,512]{1,0:T(8,128)(2,1)}, u32[]{:S(2)}) copy-start(bf16[512,512]{1,0:T(8,128)(2,1)} %param.17) | copy-start | bytes 1572868
  7.2 74.8 %all-gather.5.cloned.1.call-start = ((), (), s32[]{:S(2)}) async-start(), calls=%async_computation.7 | async-start | bytes 5406720 | tf_op jit(solution)/shard_map/all_gather | solution.py:64
  8.9 27.4 %copy-start.5 = (bf16[2048,160]{0,1:T(8,128)(2,1)S(1)}, bf16[2048,160]{0,1:T(8,128)(2,1)}, u32[]{:S(2)}) copy-start(bf16[2048,160]{0,1:T(8,128)(2,1)} %param.10) | copy-start | bytes 1966084
  15.9 18.2 %all-to-all-start.2 = ((bf16[32,1,16,512]{3,2,1,0:T(8,128)(2,1)}), bf16[32,1,16,512]{3,2,1,0:T(8,128)(2,1)S(1)}, u32[]{:S(2)}, u32[]{:S(2)}) async-start(bf16[32,1,16,512]{3,2,1,0:T(8,128)(2,1)} %fusion.5), calls=%async_computation.4 | async-start | bytes 1048576 | tf_op jit(solution)/shard_map/all_to_all | solution.py:96
  23.5 90.2 %all-gather.9.cloned.1.call-start = ((), (), s32[]{:S(2)}) async-start(), calls=%async_computation.11 | async-start | bytes 2359296 | tf_op jit(solution)/shard_map/all_gather | solution.py:100
  35.6 130.8 %all-gather.7.cloned.1.call-start = ((), (), s32[]{:S(2)}) async-start(), calls=%async_computation.9 | async-start | bytes 2703360 | tf_op jit(solution)/shard_map/all_gather | solution.py:76
  38.1 7.6 %copy-start.8 = (bf16[160]{0:T(256)(128)(2,1)S(1)}, bf16[160]{0:T(256)(128)(2,1)}, u32[]{:S(2)}) copy-start(bf16[160]{0:T(256)(128)(2,1)} %param.11) | copy-start | bytes 964
  39.3 26.1 %all-to-all-start = ((bf16[32,1,64,160]{3,2,1,0:T(8,128)(2,1)}), bf16[32,1,64,160]{3,2,1,0:T(8,128)(2,1)S(1)}, u32[]{:S(2)}, u32[]{:S(2)}) async-start(bf16[32,1,64,160]{3,2,1,0:T(8,128)(2,1)} %fusion.3), calls=%async_computation | async-start | bytes 2097152 | tf_op jit(solution)/shard_map/all_to_all | solution.py:54
  45.7 161.5 %reduce-scatter.7.cloned.1.call-start = ((), (), s32[]{:S(2)}) async-start(), calls=%async_computation.8 | async-start | bytes 1474560 | tf_op jit(solution)/shard_map/reduce_scatter | solution.py:69
  66.0 20.9 %copy-start.1 = (bf16[16,64,160]{2,1,0:T(8,128)(2,1)}, bf16[16,64,160]{2,1,0:T(8,128)(2,1)S(1)}, u32[]{:S(2)}) copy-start(bf16[16,64,160]{2,1,0:T(8,128)(2,1)S(1)} %gather_fusion.2) | copy-start | bytes 983044
  81.9 5.1 %copy-start.6 = (bf16[320]{0:T(512)(128)(2,1)S(1)}, bf16[320]{0:T(512)(128)(2,1)}, u32[]{:S(2)}) copy-start(bf16[320]{0:T(512)(128)(2,1)} %param.13) | copy-start | bytes 1924
  86.9 162.2 %all-gather.11.cloned.1.call-start = ((), (), s32[]{:S(2)}) async-start(), calls=%async_computation.12 | async-start | bytes 1474560 | tf_op jit(solution)/shard_map/all_gather | solution.py:119
  166.3 44.9 %copy-start.3 = (bf16[4096,320]{0,1:T(8,128)(2,1)S(1)}, bf16[4096,320]{0,1:T(8,128)(2,1)}, u32[]{:S(2)}) copy-start(bf16[4096,320]{0,1:T(8,128)(2,1)} %all-gather.7.cloned.1.call-done) | copy-start | bytes 7864324
  207.2 4.1 copy-start.4
  211.2 81.4 %reduce-scatter.9.cloned.1.call-start = ((), (), s32[]{:S(2)}) async-start(), calls=%async_computation.10 | async-start | bytes 2359296 | tf_op jit(solution)/shard_map/reduce_scatter | solution.py:80
  214.0 170.7 %reduce-scatter.13.cloned.1.call-start = ((), (), s32[]{:S(2)}) async-start(), calls=%async_computation.14 | async-start | bytes 3244032
  219.4 1.0 copy-start.2
  219.4 257.6 %reduce-scatter.11.cloned.1.call-start = ((), (), s32[]{:S(2)}) async-start(), calls=%async_computation.13 | async-start | bytes 3379200 | tf_op jit(solution)/shard_map/reduce_scatter | solution.py:121
  253.4 0.7 copy-start.7
  295.1 91.2 %all-to-all-start.1 = ((bf16[32,1,16,512]{3,2,1,0:T(8,128)(2,1)}), bf16[32,1,16,512]{3,2,1,0:T(8,128)(2,1)S(1)}, u32[]{:S(2)}, u32[]{:S(2)}) async-start(bf16[32,1,16,512]{3,2,1,0:T(8,128)(2,1)} %fusion.4), calls=%async_computation.3 | async-start | bytes 1048576 | tf_op jit(solution)/shard_map/all_to_all | solution.py:87
Sparse Core Ops, SparseCore 0:
  11.2 61.8 all-gather.4
  74.9 38.8 all-gather.8
  116.2 50.0 all-gather.6
  168.7 38.3 reduce-scatter.6
  211.3 37.8 all-gather.10
  251.5 40.9 reduce-scatter.8
  296.5 88.1 reduce-scatter.12
  389.3 87.5 reduce-scatter.10
where the time goes:
time: 488 us; the launch traced here: 486 us
  waiting for transfers between devices  386 us (79%)
  starting transfers between devices  21.4 us (4%)
  local copies, waits for them, and re-layouts  18.7 us (4%)
  matrix products  18.4 us (4%)
  blocking collectives  14.8 us (3%)
  between operations  14.5 us (3%)
  other arithmetic  11.8 us (2%)
    reduce_scatter x1, waiting for transfers between devices, on_device(): lax.psum_scatter(lax.dot_general(columns, merged, (((0,), (0,)), ((), ())...  89.1 us
    unnamed x9, waiting for transfers between devices  81.3 us
    all_gather x1, waiting for transfers between devices, on_device(): lax.all_gather(w_second, 'dp', axis=0, tiled=True)  52.6 us
    reduce_scatter x1, waiting for transfers between devices, on_device(): lax.psum_scatter(partial_hidden.astype(jnp.bfloat16), 'tensor', scatter_d...  40.8 us
    reduce_scatter x1, waiting for transfers between devices, on_device(): lax.psum_scatter(partial_embed.astype(jnp.bfloat16), 'tensor', scatter_di...  38.4 us
    all_gather x1, waiting for transfers between devices, on_device(): grad_pre_full = lax.all_gather(grad_pre, 'tensor', axis=1, tiled=True)  27.8 us
    all_gather x1, waiting for transfers between devices, on_device(): lax.all_gather(grad_local.reshape(tokens_here, out_width), 'tensor', axis...  26.8 us
    all_to_all x1, waiting for transfers between devices, on_device(): lax.all_to_all(outgoing, 'dp', split_axis=0, concat_axis=0, tiled=True)  19.6 us
  transfers between devices with their start and end apart: 11, of which 9 were waited for; matrix products, arithmetic and copies ran while one was open for 8% of the time, Pallas kernels for 0%

commit v1 on v0

v1 whole, which is shorter than its diff:
```python
import functools

import jax
import jax.numpy as jnp
from jax import lax
from jax.experimental import pallas as pl
from jax.experimental.pallas import tpu as pltpu
from jax.sharding import PartitionSpec as P

D = 1280
PATCH = 64
DP = 32
TP = 8
CHIPS = 16
SLOTS = 32
ROWS = PATCH // 4
TOK = 512
UNITS = 160
FEAT = 640
OUTW = 512
W1A = 48

MESH = pl.DeviceIdType.MESH
BF = jnp.bfloat16
F32 = jnp.float32
NT = (((1,), (1,)), ((), ()))
NN = (((1,), (0,)), ((), ()))
TN = (((0,), (0,)), ((), ()))


def dot(a, b, dims):
    return lax.dot_general(a, b, dims, preferred_element_type=F32)


def up(index, size):
    return lax.rem(index + size, size)


class Copies:
    def __init__(self, send, recv):
        self.send, self.recv, self.used, self.open = send, recv, 0, []

    def take(self, count):
        base = self.used
        self.used += count
        return base

    def make(self, src, dst, sem, dev, sent=None):
        return pltpu.make_async_remote_copy(
            src_ref=src,
            dst_ref=dst,
            send_sem=self.send.at[sem if sent is None else sent],
            recv_sem=self.recv.at[sem],
            device_id=dev,
            device_id_type=MESH,
        )

    def start(self, src, dst, sem, dev):
        copy = self.make(src, dst, sem, dev)
        copy.start()
        self.open.append(copy)

    def landed(self, dst, sem, dev):
        self.make(dst, dst, sem, dev).wait_recv()

    def finish(self):
        for item in self.open:
            if callable(item):
                item()
            else:
                item.wait_send()


def kernel(
    counts, pk, w1, w2p, b1, b2, gain, cot,
    emb, gw1, gw2,
    send, recv, lsem, starts, ends, srcs,
    sc, cc, g, nrm, sp, cp, x, sqx,
    w1f, w2t,
    pg, ph, zgr, zgl, zhr, zhl, og, oh,
    ht, gt,
    pe, ps, pr, sb, bk,
    g2, a2, c2, s2a, s2b, d2, e2, t2,
    g1, a1, c1, s1a, s1b, d1, e1,
):
    r = lax.axis_index("dp")
    t = lax.axis_index("tensor")
    m, c = lax.div(r, 2), lax.rem(r, 2)
    X, Y = lax.rem(m, 4), lax.div(m, 4)
    a, b = lax.div(m, 2), lax.rem(m, 2)
    links = Copies(send, recv)

    def plane(chip):
        return (2 * chip + c, t)

    def along_x(d):
        return plane(4 * Y + up(X + d, 4))

    def along_y(d):
        return plane(4 * up(Y + d, 4) + X)

    sibling = (2 * m + 1 - c, t)
    right, left = (r, up(t + 1, TP)), (r, up(t - 1, TP))
    mate = 2 * t + b
    same = a == t

    barrier = pltpu.get_barrier_semaphore()

    def greet(dev):
        pl.semaphore_signal(barrier, inc=1, device_id=dev, device_id_type=MESH)

    for d in range(1, CHIPS):
        greet(plane(up(m + d, CHIPS)))
    for d in range(1, TP):
        greet((r, up(t + d, TP)))
    greet(sibling)

    @pl.when(jnp.logical_not(same))
    def _():
        for e in range(2):
            greet((2 * mate + e, a))

    def prefix(s, total):
        starts[s] = total
        total = total + counts[s]
        ends[s] = total
        return total

    lax.fori_loop(0, DP, prefix, jnp.int32(0))
    mine_start, mine_count = starts[r], counts[r]

    def pack_cot(p, carry):
        sc[p] = cot[up(p - mine_start + 1024, SLOTS)]
        return carry

    lax.fori_loop(0, DP, pack_cot, 0)

    lane = lax.broadcasted_iota(jnp.int32, (8, FEAT), 1)
    row = lax.broadcasted_iota(jnp.int32, (8, FEAT), 0)
    lead = jnp.logical_and(lane >= row * 160, lane < row * 160 + 160)
    pick = jnp.where(lead, 1.0, 0.0).astype(F32)
    pick_bf = pick.astype(BF)
    for i in range(4):
        v = pk[8 * i : 8 * i + 8].reshape(128, FEAT).astype(F32)
        sq = v * v
        high = sq.astype(BF)
        low = (sq - high.astype(F32)).astype(BF)
        sqx[t, :, 128 * i : 128 * i + 128] = dot(pick_bf, high, NT) + dot(pick_bf, low, NT)

    w1f[Y, X] = w1[...]

    pl.semaphore_wait(barrier, 23 + jnp.where(same, 0, 2))

    relay = links.take(2)
    relay_out = w2t.at[
        lax.div(t, 2), lax.rem(t, 2), :, pl.ds(pl.multiple_of(b * 256 + c * 128, 128), 128)
    ]

    def relay_in(e):
        return w2t.at[
            lax.div(a, 2), lax.rem(a, 2), :, pl.ds(pl.multiple_of(b * 256 + e * 128, 128), 128)
        ]

    @pl.when(jnp.logical_not(same))
    def _():
        for e in range(2):
            links.make(w2p.at[e], relay_out, relay + c, (2 * mate + e, a), relay + e).start()

    @pl.when(same)
    def _():
        links.make(w2p.at[1 - c], relay_out, relay + c, sibling, relay + 1 - c).start()
        own = pltpu.make_async_copy(w2p.at[c], relay_out, lsem)
        own.start()
        own.wait()

    def relay_sent():
        @pl.when(jnp.logical_not(same))
        def _():
            for e in range(2):
                links.make(w2p.at[e], relay_out, relay + c, (2 * mate + e, a), relay + e).wait_send()

        @pl.when(same)
        def _():
            links.make(w2p.at[1 - c], relay_out, relay + c, sibling, relay + 1 - c).wait_send()

    links.open.append(relay_sent)

    def exchange(out, into, base):
        def step(d, carry):
            chip = up(m + d, CHIPS)
            links.make(out.at[pl.ds(2 * chip, 2)], into.at[m], base + d, plane(chip)).start()
            return carry

        lax.fori_loop(1, CHIPS, step, 0)

        def sent(d, carry):
            chip = up(m + d, CHIPS)
            links.make(out.at[pl.ds(2 * chip, 2)], into.at[m], base + d, plane(chip)).wait_send()
            return carry

        links.open.append(lambda: lax.fori_loop(1, CHIPS, sent, 0))
        into[m] = out[pl.ds(2 * m, 2)]

    def exchanged(into, base):
        def step(d, carry):
            links.landed(into.at[up(m - d, CHIPS)], base + d, plane(up(m - d, CHIPS)))
            return carry

        lax.fori_loop(1, CHIPS, step, 0)

    cot_base = links.take(CHIPS)
    exchange(sc, cc.at[c], cot_base)

    sq_base = links.take(TP)
    for d in range(1, TP):
        links.start(sqx.at[t], sqx.at[t], sq_base + d, (r, up(t + d, TP)))

    def gather_first(block_a, block_b, base):
        for d in range(1, 4):
            links.start(block_a, block_a, base + d, along_x(d))
            links.start(block_b, block_b, base + 3 + d, along_y(d))

    w1a = w1f.at[Y, X, 0:W1A]
    w1b = w1f.at[Y, X, W1A:80]
    w1_base = links.take(16)
    w2_base = links.take(16)
    w2lane = pl.ds(pl.multiple_of(b * 256, 256), 256)
    xh = lax.div(X, 2)
    w2a = w2t.at[Y, xh, 0:80, w2lane]
    w2b = w2t.at[Y, xh, 80:160, w2lane]

    def source(k, carry):
        p0 = 32 * k + 2 * m
        n0, n1 = jnp.int32(0), jnp.int32(0)
        for s in range(DP):
            v = ends[s]
            n0 = n0 + (v <= p0).astype(jnp.int32)
            n1 = n1 + (v <= p0 + 1).astype(jnp.int32)
        srcs[k] = jnp.minimum(n0, DP - 1)
        srcs[16 + k] = jnp.minimum(n1, DP - 1)
        return carry

    lax.fori_loop(0, 16, source, 0)

    for e in range(2):

        @pl.when(jnp.logical_or(jnp.logical_not(same), e != c))
        def _(e=e):
            links.landed(relay_in(e), relay + e, sibling)

    gather_first(w2a, w2b, w2_base)

    for d in range(1, TP):
        z = up(t - d, TP)
        links.landed(sqx.at[z], sq_base + d, (r, z))
    total = sqx[0]
    for z in range(1, TP):
        total = total + sqx[z]
    inv = lax.rsqrt(total / D + 1e-06)
    i1 = inv.astype(BF).astype(F32)
    i2 = (inv - i1).astype(BF).astype(F32)
    i3 = (inv - i1) - i2
    stack = jnp.concatenate([i1, i2, i3], axis=0)
    stack_t = stack.T.astype(BF)
    pick3 = jnp.concatenate([pick, pick, pick], axis=0).astype(BF)
    gains = gain[...]
    for i in range(4):
        scale = dot(stack_t[128 * i : 128 * i + 128], pick3, NN)
        v = pk[8 * i : 8 * i + 8].reshape(128, FEAT).astype(F32)
        nrm[8 * i : 8 * i + 8] = (v * scale * gains).astype(BF).reshape(8, ROWS, FEAT)

    def pack_rows(p, carry):
        sp[p] = nrm[up(p - mine_start + 1024, SLOTS)]
        return carry

    lax.fori_loop(0, DP, pack_rows, 0)
    row_base = links.take(CHIPS)
    exchange(sp, cp.at[c], row_base)
    gather_first(w1a, w1b, w1_base)

    def gather_second(wide_a, wide_b, arrived, base):
        for d in range(1, 4):
            ra, rb = arrived(d)
            links.landed(ra, base + d, along_x(-d))
            links.landed(rb, base + 3 + d, along_y(-d))
        for d in range(1, 4):
            links.start(wide_a, wide_a, base + 6 + d, along_y(d))
            links.start(wide_b, wide_b, base + 9 + d, along_x(d))

    def w2_first(d):
        xx, yy = up(X - d, 4), up(Y - d, 4)
        ra = w2t.at[Y, lax.div(xx, 2), 0:80, pl.ds(pl.multiple_of(lax.rem(xx, 2) * 256, 256), 256)]
        rb = w2t.at[yy, xh, 80:160, w2lane]
        return ra, rb

    def w1_first(d):
        return w1f.at[Y, up(X - d, 4), 0:W1A], w1f.at[up(Y - d, 4), X, W1A:80]

    gather_second(w2t.at[Y, :, 0:80], w2t.at[:, xh, 80:160, w2lane], w2_first, w2_base)

    exchanged(cc.at[c], cot_base)
    cot_sib = links.take(1)
    links.start(cc.at[c], cc.at[c], cot_sib, sibling)

    gather_second(w1f.at[Y, :, 0:W1A], w1f.at[:, X, W1A:80], w1_first, w1_base)

    links.landed(cc.at[1 - c], cot_sib, sibling)

    def choose(cand, out):
        def step(j, carry):
            s = srcs[j]
            out[j] = cand[lax.rem(s, 2), lax.div(s, 2), lax.div(j, 16)]
            return carry

        lax.fori_loop(0, 32, step, 0)

    choose(cc, g)

    for d in range(1, 4):
        xx, yy = up(X - d, 4), up(Y - d, 4)
        links.landed(w2t.at[yy, :, 0:80], w2_base + 6 + d, along_y(-d))
        links.landed(
            w2t.at[:, lax.div(xx, 2), 80:160, pl.ds(pl.multiple_of(lax.rem(xx, 2) * 256, 256), 256)],
            w2_base + 9 + d,
            along_x(-d),
        )

    def ring_sum(part, rr, rl, base, s):
        br, bl = up(t + 4 - s, TP), up(t - 4 + s, TP)
        if s == 0:
            links.start(part.at[br, 0:80], rr.at[0, 0:80], base, right)
            links.start(part.at[bl, 80:160], rl.at[0, 80:160], base + 4, left)
            return
        lo, hi = ((0, 80), (80, 160)) if s == 1 else ((0, 160), (0, 160))
        links.landed(rr.at[s - 1, lo[0] : lo[1]], base + s - 1, left)
        part[br, lo[0] : lo[1]] = (
            part[br, lo[0] : lo[1]].astype(F32) + rr[s - 1, lo[0] : lo[1]].astype(F32)
        ).astype(BF)
        links.start(part.at[br], rr.at[s], base + s, right)
        links.landed(rl.at[s - 1, hi[0] : hi[1]], base + 4 + s - 1, right)
        part[bl, hi[0] : hi[1]] = (
            part[bl, hi[0] : hi[1]].astype(F32) + rl[s - 1, hi[0] : hi[1]].astype(F32)
        ).astype(BF)
        links.start(part.at[bl], rl.at[s], base + 4 + s, left)

    def ring_end(rr, rl, base):
        links.landed(rr.at[3], base + 3, left)
        links.landed(rl.at[3], base + 7, right)

    def grad_block(z):
        gg = g[...].reshape(TOK, OUTW)
        return dot(w2t[lax.div(z, 2), lax.rem(z, 2)], gg, NT)

    def grad_blocks(i, carry):
        z = up(t + 4 + i, TP)
        pg[z] = grad_block(z).astype(BF)
        return carry

    pg_base = links.take(8)
    lax.fori_loop(0, 1, grad_blocks, 0)
    ring_sum(pg, zgr, zgl, pg_base, 0)
    lax.fori_loop(1, 8, grad_blocks, 0)
    og[...] = grad_block(t)
    ring_sum(pg, zgr, zgl, pg_base, 1)

    exchanged(cp.at[c], row_base)
    row_sib = links.take(1)
    links.start(cp.at[c], cp.at[c], row_sib, sibling)
    ring_sum(pg, zgr, zgl, pg_base, 2)
    links.landed(cp.at[1 - c], row_sib, sibling)
    choose(cp, x)
    ring_sum(pg, zgr, zgl, pg_base, 3)

    for d in range(1, 4):
        xx, yy = up(X - d, 4), up(Y - d, 4)
        links.landed(w1f.at[yy, :, 0:W1A], w1_base + 6 + d, along_y(-d))
        links.landed(w1f.at[:, xx, W1A:80], w1_base + 9 + d, along_x(-d))

    def pre_block(z):
        rows = w1f[lax.div(z, 2), pl.ds(2 * lax.rem(z, 2), 2)].reshape(UNITS, FEAT)
        return dot(rows, x[...].reshape(TOK, FEAT), NT)

    def pre_blocks(i, carry):
        z = up(t + 4 + i, TP)
        ph[z] = pre_block(z).astype(BF)
        return carry

    ph_base = links.take(8)
    lax.fori_loop(0, 1, pre_blocks, 0)
    ring_sum(ph, zhr, zhl, ph_base, 0)
    lax.fori_loop(1, 8, pre_blocks, 0)
    oh[...] = pre_block(t)
    for s in range(1, 4):
        ring_sum(ph, zhr, zhl, ph_base, s)
    ring_end(zgr, zgl, pg_base)
    ring_end(zhr, zhl, ph_base)

    def activate(i, carry):
        rows = pl.ds(pl.multiple_of(i * 32, 32), 32)
        bias = b1[c, rows]
        v = oh[rows] + zhr[3, rows].astype(F32) + zhl[3, rows].astype(F32)
        v = v + jnp.concatenate([bias] * 4, axis=1)
        cdf = 0.5 * (1.0 + lax.erf(v * 0.7071067811865476))
        density = jnp.exp(-0.5 * v * v) * 0.3989422804014327
        ht[t, rows] = (v * cdf).astype(BF)
        gh = og[rows] + zgr[3, rows].astype(F32) + zgl[3, rows].astype(F32)
        gt[t, rows] = (gh * (cdf + v * density)).astype(BF)
        return carry

    lax.fori_loop(0, 5, activate, 0)

    def ring_copy(buf, base, s):
        br, bl = up(t - s, TP), up(t + s, TP)
        if s > 0:
            links.landed(buf.at[br], base + s - 1, left)
            links.landed(buf.at[bl], base + 4 + s - 1, right)
        if s < 3:
            links.start(buf.at[br], buf.at[br], base + s, right)
            links.start(buf.at[bl], buf.at[bl], base + 4 + s, left)
        else:
            links.start(buf.at[br, 0:80], buf.at[br, 0:80], base + s, right)
            links.start(buf.at[bl, 80:160], buf.at[bl, 80:160], base + 4 + s, left)

    def ring_copied(buf, base):
        far = up(t + 4, TP)
        links.landed(buf.at[far, 0:80], base + 3, left)
        links.landed(buf.at[far, 80:160], base + 7, right)

    ht_base, gt_base = links.take(8), links.take(8)
    ring_copy(ht, ht_base, 0)
    ring_copy(gt, gt_base, 0)
    ring_copy(ht, ht_base, 1)
    ring_copy(gt, gt_base, 1)
    ring_copy(ht, ht_base, 2)
    ring_copy(ht, ht_base, 3)
    ring_copy(gt, gt_base, 2)
    ring_copied(ht, ht_base)

    def plane_sum_first(part, cut, ra, rb, base):
        for d in range(1, 4):
            yy, xx = up(Y + d, 4), up(X + d, 4)
            links.start(part.at[yy, :, 0:cut], ra.at[d - 1], base + d, along_y(d))
            links.start(part.at[:, xx, cut:], rb.at[d - 1], base + 3 + d, along_x(d))

    def plane_sum_second(part, cut, ra, rb, sa, sbx, rc, rd, base):
        for d in range(1, 4):
            links.landed(ra.at[d - 1], base + d, along_y(-d))
        for i in range(4):
            v = part[Y, i, 0:cut].astype(F32)
            for d in range(3):
                v = v + ra[d, i].astype(F32)
            sa[i] = v.astype(BF)
        for d in range(1, 4):
            links.start(sa.at[up(X + d, 4)], rc.at[d - 1], base + 6 + d, along_x(d))
        for d in range(1, 4):
            links.landed(rb.at[d - 1], base + 3 + d, along_x(-d))
        for i in range(4):
            v = part[i, X, cut:].astype(F32)
            for d in range(3):
                v = v + rb[d, i].astype(F32)
            sbx[i] = v.astype(BF)
        for d in range(1, 4):
            links.start(sbx.at[up(Y + d, 4)], rd.at[d - 1], base + 9 + d, along_y(d))

    def plane_sum_end(sa, sbx, rc, rd, base):
        for d in range(1, 4):
            links.landed(rc.at[d - 1], base + 6 + d, along_x(-d))
        va = sa[X].astype(F32)
        for d in range(3):
            va = va + rc[d].astype(F32)
        for d in range(1, 4):
            links.landed(rd.at[d - 1], base + 9 + d, along_y(-d))
        vb = sbx[Y].astype(F32)
        for d in range(3):
            vb = vb + rd[d].astype(F32)
        return va.astype(BF), vb.astype(BF)

    def second_grad(z, carry):
        v = dot(ht[z], g[...].reshape(TOK, OUTW), NN).astype(BF)
        for i in range(2):
            g2[lax.div(z, 2), 2 * lax.rem(z, 2) + i] = v[:, 256 * i : 256 * i + 256]
        return carry

    lax.fori_loop(0, TP, second_grad, 0)
    g2_base = links.take(16)
    plane_sum_first(g2, 80, a2, c2, g2_base)

    def embed(i, carry):
        lanes = pl.ds(pl.multiple_of(i * 128, 128), 128)
        acc = jnp.zeros((128, OUTW), F32)
        for z in range(TP):
            acc = acc + dot(ht[z, :, lanes].astype(F32).T.astype(BF), w2t[z // 2, z % 2], NN)
        pe[pl.ds(8 * i, 8)] = acc.reshape(8, ROWS, OUTW)
        return carry

    lax.fori_loop(0, 4, embed, 0)
    ring_copy(gt, gt_base, 3)

    def window_of(s, e):
        first = starts[s]
        slot = lax.rem(2 * m + e - first + 1024, SLOTS)
        return e * 16 + jnp.minimum(lax.div(first + slot, 32), 15)

    def pack_sibling(i, carry):
        for e in range(2):
            ps[2 * i + e] = pe[window_of(2 * i + 1 - c, e)].astype(BF)
        return carry

    lax.fori_loop(0, CHIPS, pack_sibling, 0)
    emb_sib = links.take(1)
    links.start(ps, pr, emb_sib, sibling)
    plane_sum_second(g2, 80, a2, c2, s2a, s2b, d2, e2, g2_base)
    links.landed(pr, emb_sib, sibling)
    bias2 = b2[...]

    def pack_home(i, carry):
        for e in range(2):
            v = pe[window_of(2 * i + c, e)] + pr[2 * i + e].astype(F32) + bias2
            sb[2 * i + e] = v.astype(BF)
        return carry

    lax.fori_loop(0, CHIPS, pack_home, 0)
    home_base = links.take(CHIPS)
    exchange(sb, bk, home_base)

    ring_copied(gt, gt_base)

    def first_grad(z, carry):
        v = dot(gt[z], x[...].reshape(TOK, FEAT), NN).astype(BF)
        for i in range(2):
            g1[lax.div(z, 2), 2 * lax.rem(z, 2) + i] = v[80 * i : 80 * i + 80]
        return carry

    lax.fori_loop(0, TP, first_grad, 0)
    g1_base = links.take(16)
    plane_sum_first(g1, W1A, a1, c1, g1_base)

    va, vb = plane_sum_end(s2a, s2b, d2, e2, g2_base)
    for e in range(2):
        t2[e, 0:80] = va[:, 128 * e : 128 * e + 128]
        t2[e, 80:160] = vb[:, 128 * e : 128 * e + 128]
    back = links.take(2)

    @pl.when(jnp.logical_not(same))
    def _():
        for e in range(2):
            links.make(t2.at[e], gw2.at[c], back + c, (2 * mate + e, a), back + e).start()

    @pl.when(same)
    def _():
        links.make(t2.at[1 - c], gw2.at[c], back + c, sibling, back + 1 - c).start()
        gw2[c] = t2[c]

    def back_sent():
        @pl.when(jnp.logical_not(same))
        def _():
            for e in range(2):
                links.make(t2.at[e], gw2.at[c], back + c, (2 * mate + e, a), back + e).wait_send()

        @pl.when(same)
        def _():
            links.make(t2.at[1 - c], gw2.at[c], back + c, sibling, back + 1 - c).wait_send()

    links.open.append(back_sent)

    plane_sum_second(g1, W1A, a1, c1, s1a, s1b, d1, e1, g1_base)

    exchanged(bk, home_base)

    def home(j, carry):
        p = lax.rem(mine_start + j, DP)
        v = bk[lax.div(p, 2), lax.rem(p, 2)].astype(F32)
        emb[j] = jnp.where(j < mine_count, v, 0.0).astype(BF)
        return carry

    lax.fori_loop(0, SLOTS, home, 0)

    for e in range(2):

        @pl.when(jnp.logical_or(jnp.logical_not(same), e != c))
        def _(e=e):
            links.landed(gw2.at[e], back + e, sibling)

    va, vb = plane_sum_end(s1a, s1b, d1, e1, g1_base)
    gw1[0:W1A] = va
    gw1[W1A:80] = vb
    links.finish()


def on_device(patches, norm_gain, w_first, b_first, w_second, b_second, counts, cotangent):
    pk = patches.reshape(SLOTS, ROWS, FEAT)
    w1 = w_first.reshape(80, FEAT)
    w2p = w_second.T.reshape(2, 2, 80, 128).transpose(1, 0, 2, 3).reshape(2, UNITS, 128)
    b1 = b_first.astype(F32).reshape(2, 2, 80).transpose(1, 0, 2).reshape(2, UNITS, 1)
    b1 = jnp.broadcast_to(b1, (2, UNITS, 128))
    b2 = b_second.astype(F32).reshape(1, OUTW)
    gain = jnp.tile(norm_gain.astype(F32).reshape(1, 160), (1, 4))
    cot = cotangent.reshape(SLOTS, ROWS, OUTW)

    vmem = pl.BlockSpec(memory_space=pltpu.VMEM)
    V = pltpu.VMEM
    S = pltpu.SMEM
    emb, gw1, gw2 = pl.pallas_call(
        kernel,
        name="merger",
        out_shape=(
            jax.ShapeDtypeStruct((SLOTS, ROWS, OUTW), BF),
            jax.ShapeDtypeStruct((80, FEAT), BF),
            jax.ShapeDtypeStruct((2, UNITS, 128), BF),
        ),
        in_specs=[pl.BlockSpec(memory_space=pltpu.SMEM)] + [vmem] * 7,
        out_specs=(vmem, vmem, vmem),
        scratch_shapes=[
            pltpu.SemaphoreType.DMA((200,)),
            pltpu.SemaphoreType.DMA((200,)),
            pltpu.SemaphoreType.DMA,
            S((DP,), jnp.int32),
            S((DP,), jnp.int32),
            S((DP,), jnp.int32),
            V((DP, ROWS, OUTW), BF),
            V((2, CHIPS, 2, ROWS, OUTW), BF),
            V((32, ROWS, OUTW), BF),
            V((SLOTS, ROWS, FEAT), BF),
            V((DP, ROWS, FEAT), BF),
            V((2, CHIPS, 2, ROWS, FEAT), BF),
            V((32, ROWS, FEAT), BF),
            V((TP, 8, TOK), F32),
            V((4, 4, 80, FEAT), BF),
            V((4, 2, UNITS, OUTW), BF),
            V((TP, UNITS, TOK), BF),
            V((TP, UNITS, TOK), BF),
            V((4, UNITS, TOK), BF),
            V((4, UNITS, TOK), BF),
            V((4, UNITS, TOK), BF),
            V((4, UNITS, TOK), BF),
            V((UNITS, TOK), F32),
            V((UNITS, TOK), F32),
            V((TP, UNITS, TOK), BF),
            V((TP, UNITS, TOK), BF),
            V((32, ROWS, OUTW), F32),
            V((32, ROWS, OUTW), BF),
            V((32, ROWS, OUTW), BF),
            V((32, ROWS, OUTW), BF),
            V((CHIPS, 2, ROWS, OUTW), BF),
            V((4, 4, UNITS, 256), BF),
            V((3, 4, 80, 256), BF),
            V((3, 4, 80, 256), BF),
            V((4, 80, 256), BF),
            V((4, 80, 256), BF),
            V((3, 80, 256), BF),
            V((3, 80, 256), BF),
            V((2, UNITS, 128), BF),
            V((4, 4, 80, FEAT), BF),
            V((3, 4, W1A, FEAT), BF),
            V((3, 4, 80 - W1A, FEAT), BF),
            V((4, W1A, FEAT), BF),
            V((4, 80 - W1A, FEAT), BF),
            V((3, W1A, FEAT), BF),
            V((3, 80 - W1A, FEAT), BF),
        ],
        compiler_params=pltpu.CompilerParams(
            collective_id=0, has_side_effects=True, vmem_limit_bytes=56 * 1024 * 1024
        ),
        cost_estimate=pl.CostEstimate(
            flops=3_700_000_000, bytes_accessed=3_000_000, transcendentals=200_000
        ),
    )(counts, pk, w1, w2p, b1, b2, gain, cot)
    embeddings = emb.reshape(SLOTS * ROWS, OUTW)
    grad_w1 = gw1.reshape(80, 4, 160)
    grad_w2 = gw2.reshape(2, 2, 80, 128).transpose(3, 1, 0, 2).reshape(128, 320)
    return embeddings, grad_w1, grad_w2


def solution(mesh):
    in_specs = (
        P("dp", "tensor"),
        P("tensor"),
        P("dp", None, "tensor"),
        P("tensor"),
        P("dp", "tensor"),
        P("tensor"),
        P(),
        P("dp", "tensor"),
    )
    out_specs = (P("dp", "tensor"), P("dp", None, "tensor"), P("dp", "tensor"))
    return jax.shard_map(
        on_device, mesh=mesh, in_specs=in_specs, out_specs=out_specs, check_vma=False
    )
```

time: 488 us -> 163 us (0.33)
  the two profiles are of different devices: /device:TPU:164 before, /device:TPU:6 now
where the time goes in v1:
time: 163 us
  Pallas kernels  150 us (92%)
  local copies, waits for them, and re-layouts  11.8 us (7%)
    pallas_call x1, Pallas kernels, on_device(): pl.pallas_call(kernel, name='merger', out_shape=(jax.ShapeDtypeStruct((SL...  150 us
    unnamed x14, local copies, waits for them, and re-layouts  4.06 us

profile of v1, /device:TPU:6, one launch (start us, length us, event | category | flops | bytes accessed | tf_op | source)
XLA Modules:
  0.0 162.8 jit_solution(7666291582797143813)
XLA Ops:
  0.6 1.4 copy.17
  2.0 0.0 copy-start.3
  2.1 2.3 %reshape.50.pk = bf16[32,16,640]{2,1,0:T(8,128)(2,1)} reshape(bf16[2048,160]{1,0:T(8,128)(2,1)S(1)} %copy.17) | data formatting | bytes 1310720 | tf_op jit(solution)/shard_map/reshape | solution.py:591
  4.4 0.0 copy-done.3
  4.4 0.0 copy-start
  4.4 0.1 reshape.65
  4.5 0.1 reshape.62
  4.6 0.8 broadcast_in_dim.12.b1
  5.4 0.0 copy-done
  5.4 0.0 copy-start.1
  5.4 0.8 reshape.51.w1
  6.2 0.1 copy-done.1
  6.3 0.6 copy.18
  6.9 0.0 copy-start.5
  6.9 0.7 copy-done.5
  7.6 0.0 copy-start.4
  7.6 0.7 tile.9.gain
  8.2 0.0 copy-done.4
  8.2 0.6 reshape.63
  8.8 149.7 %merger.1 = (bf16[32,16,512]{2,1,0:T(8,128)(2,1)}, bf16[80,640]{1,0:T(8,128)(2,1)}, bf16[2,160,128]{2,1,0:T(8,128)(2,1)}) custom-call(s32[32]{0:T(128)} %counts.1, bf16[32,16,640]{2,1,0:T(8,128)(2,1)} %reshape.50.pk, bf16[80,640]{1,0:T(8,128)(2,1)} %reshape.51.w1, bf16[2,160,128]{2,1,0:T(8,128)(2,1)} %bitcast.17, f32[2,160,128]{2,1,0:T(8,128)} %broadcast_in_dim.12.b1, ...), custom_call_target="tpu_custom_call" | custom-call | flops 3700000000 | bytes 3000000 | tf_op jit(solution)/shard_map/merger/pallas_call | solution.py:603
  158.6 0.0 copy-start.2
  158.6 1.8 %reshape.59 = bf16[80,4,160]{2,1,0:T(4,128)(2,1)} reshape(bf16[80,640]{1,0:T(8,128)(2,1)} %get-tuple-element.7) | data formatting | bytes 204800 | tf_op jit(solution)/shard_map/reshape | solution.py:669
  160.3 0.0 copy-done.2
  160.3 0.6 copy.20
  161.0 1.9 %copy.22 = bf16[512,512]{1,0:T(8,128)(2,1)} copy(bf16[512,512]{1,0:T(8,128)(2,1)} %bitcast.14) | data formatting | bytes 1048576
  (2 shorter events, 0.0 us)
Async XLA Ops:
  2.0 2.4 %copy-start.3 = (bf16[320]{0:T(512)(128)(2,1)S(1)}, bf16[320]{0:T(512)(128)(2,1)}, u32[]{:S(2)}) copy-start(bf16[320]{0:T(512)(128)(2,1)} %param.11) | copy-start | bytes 1924
  4.4 1.0 copy-start
  5.4 0.9 copy-start.1
  6.9 0.7 copy-start.5
  7.6 0.7 copy-start.4
  158.6 1.8 %copy-start.2 = (bf16[2,160,128]{2,1,0:T(8,128)(2,1)S(1)}, bf16[2,160,128]{2,1,0:T(8,128)(2,1)}, u32[]{:S(2)}) copy-start(bf16[2,160,128]{2,1,0:T(8,128)(2,1)} %get-tuple-element.8) | copy-start | bytes 245764

commit v2 on v1

v2 whole, which is shorter than its diff:
```python
import functools

import jax
import jax.numpy as jnp
from jax import lax
from jax.experimental import pallas as pl
from jax.experimental.pallas import tpu as pltpu
from jax.sharding import PartitionSpec as P

D = 1280
PATCH = 64
DP = 32
TP = 8
CHIPS = 16
SLOTS = 32
ROWS = PATCH // 4
TOK = 512
UNITS = 160
FEAT = 640
OUTW = 512
W1A = 48

MESH = pl.DeviceIdType.MESH
BF = jnp.bfloat16
F32 = jnp.float32
NT = (((1,), (1,)), ((), ()))
NN = (((1,), (0,)), ((), ()))
TN = (((0,), (0,)), ((), ()))


def dot(a, b, dims):
    return lax.dot_general(a, b, dims, preferred_element_type=F32)


def up(index, size):
    return lax.rem(index + size, size)


class Copies:
    def __init__(self, send, recv):
        self.send, self.recv, self.used, self.open = send, recv, 0, []

    def take(self, count):
        base = self.used
        self.used += count
        return base

    def make(self, src, dst, sem, dev, sent=None):
        return pltpu.make_async_remote_copy(
            src_ref=src,
            dst_ref=dst,
            send_sem=self.send.at[sem if sent is None else sent],
            recv_sem=self.recv.at[sem],
            device_id=dev,
            device_id_type=MESH,
        )

    def start(self, src, dst, sem, dev):
        copy = self.make(src, dst, sem, dev)
        copy.start()
        self.open.append(copy)

    def landed(self, dst, sem, dev):
        self.make(dst, dst, sem, dev).wait_recv()

    def finish(self):
        for item in self.open:
            if callable(item):
                item()
            else:
                item.wait_send()


def kernel(
    counts, pk, w1, w2p, b1, b2, gain, cot,
    emb, gw1, gw2,
    send, recv, lsem, starts, ends, srcs,
    sc, cc, g, nrm, sp, cp, xf, sqx,
    w1f, w2t,
    pg, zgr, zgl, og, oh,
    ht, gt,
    pe, ps, pr, sb, bk,
    g2, a2, c2, s2a, s2b, d2, e2, t2,
    g1, a1, c1, s1a, s1b, d1, e1, t1,
    i1, i2, k1, k2,
):
    r = lax.axis_index("dp")
    t = lax.axis_index("tensor")
    m, c = lax.div(r, 2), lax.rem(r, 2)
    X, Y = lax.rem(m, 4), lax.div(m, 4)
    a, b = lax.div(m, 2), lax.rem(m, 2)
    links = Copies(send, recv)

    def plane(chip):
        return (2 * chip + c, t)

    def along_x(d):
        return plane(4 * Y + up(X + d, 4))

    def along_y(d):
        return plane(4 * up(Y + d, 4) + X)

    sibling = (2 * m + 1 - c, t)
    right, left = (r, up(t + 1, TP)), (r, up(t - 1, TP))
    mid_chip, old_chip = lax.rem(m + 2 * t, CHIPS), up(m - 2 * t, CHIPS)
    mate = up(a - t, TP)
    same, still = mate == t, t == 0

    barrier = pltpu.get_barrier_semaphore()

    def greet(dev):
        pl.semaphore_signal(barrier, inc=1, device_id=dev, device_id_type=MESH)

    for d in range(1, CHIPS):
        greet(plane(up(m + d, CHIPS)))
    for d in range(1, TP):
        greet((r, up(t + d, TP)))
    greet(sibling)

    @pl.when(jnp.logical_not(same))
    def _():
        greet((2 * m + 1 - c, mate))

    def prefix(s, total):
        starts[s] = total
        total = total + counts[s]
        ends[s] = total
        return total

    lax.fori_loop(0, DP, prefix, jnp.int32(0))
    mine_start, mine_count = starts[r], counts[r]

    def pack_cot(p, carry):
        sc[p] = cot[up(p - mine_start + 1024, SLOTS)]
        return carry

    lax.fori_loop(0, DP, pack_cot, 0)

    lane = lax.broadcasted_iota(jnp.int32, (8, FEAT), 1)
    row = lax.broadcasted_iota(jnp.int32, (8, FEAT), 0)
    lead = jnp.logical_and(lane >= row * 160, lane < row * 160 + 160)
    pick = jnp.where(lead, 1.0, 0.0).astype(F32)
    pick_bf = pick.astype(BF)
    for i in range(4):
        v = pk[8 * i : 8 * i + 8].reshape(128, FEAT).astype(F32)
        sq = v * v
        high = sq.astype(BF)
        low = (sq - high.astype(F32)).astype(BF)
        sqx[t, :, 128 * i : 128 * i + 128] = dot(pick_bf, high, NT) + dot(pick_bf, low, NT)

    pl.semaphore_wait(barrier, 23 + jnp.where(same, 0, 1))

    sq_base = links.take(TP)
    for d in range(1, TP):
        links.start(sqx.at[t], sqx.at[t], sq_base + d, (r, up(t + d, TP)))

    relay = links.take(2)
    relay1 = links.take(1)
    relay_mid = links.take(2)

    def relay_in(e):
        return w2t.at[Y, lax.div(X, 2), :, pl.ds(pl.multiple_of(b * 256 + e * 128, 128), 128)]

    def relay_steps(do):
        @pl.when(jnp.logical_not(still))
        def _():
            do(links.make(w2p, i2, relay_mid, plane(mid_chip)))
            do(links.make(w1, i1, relay_mid + 1, plane(mid_chip)))

    def relay_along_z(do):
        @pl.when(jnp.logical_not(same))
        def _():
            for e in range(2):
                do(links.make(i2.at[e], relay_in(c), relay + c, (2 * m + e, mate), relay + e))
            do(links.make(i1, w1f.at[Y, X], relay1, (r, mate)))

        @pl.when(same)
        def _():
            do(links.make(i2.at[1 - c], relay_in(c), relay + c, sibling, relay + 1 - c))

    relay_steps(lambda copy: copy.start())

    @pl.when(still)
    def _():
        i2[...] = w2p[...]
        i1[...] = w1[...]

    links.open.append(lambda: relay_steps(lambda copy: copy.wait_send()))
    links.open.append(lambda: relay_along_z(lambda copy: copy.wait_send()))

    def exchange(out, into, base):
        def step(d, carry):
            chip = up(m + d, CHIPS)
            links.make(out.at[pl.ds(2 * chip, 2)], into.at[m], base + d, plane(chip)).start()
            return carry

        lax.fori_loop(1, CHIPS, step, 0)

        def sent(d, carry):
            chip = up(m + d, CHIPS)
            links.make(out.at[pl.ds(2 * chip, 2)], into.at[m], base + d, plane(chip)).wait_send()
            return carry

        links.open.append(lambda: lax.fori_loop(1, CHIPS, sent, 0))
        into[m] = out[pl.ds(2 * m, 2)]

    def exchanged(into, base):
        def step(d, carry):
            links.landed(into.at[up(m - d, CHIPS)], base + d, plane(up(m - d, CHIPS)))
            return carry

        lax.fori_loop(1, CHIPS, step, 0)


    def gather_first(block_a, block_b, base):
        for d in range(1, 4):
            links.start(block_a, block_a, base + d, along_x(d))
            links.start(block_b, block_b, base + 3 + d, along_y(d))

    w1a = w1f.at[Y, X, 0:W1A]
    w1b = w1f.at[Y, X, W1A:80]
    w1_base = links.take(16)
    w2_base = links.take(16)
    w2lane = pl.ds(pl.multiple_of(b * 256, 256), 256)
    xh = lax.div(X, 2)
    w2a = w2t.at[Y, xh, 0:80, w2lane]
    w2b = w2t.at[Y, xh, 80:160, w2lane]

    def gather_second(wide_a, wide_b, arrived, base):
        for d in range(1, 4):
            ra, rb = arrived(d)
            links.landed(ra, base + d, along_x(-d))
            links.landed(rb, base + 3 + d, along_y(-d))
        for d in range(1, 4):
            links.start(wide_a, wide_a, base + 6 + d, along_y(d))
            links.start(wide_b, wide_b, base + 9 + d, along_x(d))

    def w2_first(d):
        xx, yy = up(X - d, 4), up(Y - d, 4)
        ra = w2t.at[Y, lax.div(xx, 2), 0:80, pl.ds(pl.multiple_of(lax.rem(xx, 2) * 256, 256), 256)]
        rb = w2t.at[yy, xh, 80:160, w2lane]
        return ra, rb

    def w1_first(d):
        return w1f.at[Y, up(X - d, 4), 0:W1A], w1f.at[up(Y - d, 4), X, W1A:80]

    def source(k, carry):
        p0 = 32 * k + 2 * m
        n0, n1 = jnp.int32(0), jnp.int32(0)
        for s in range(DP):
            v = ends[s]
            n0 = n0 + (v <= p0).astype(jnp.int32)
            n1 = n1 + (v <= p0 + 1).astype(jnp.int32)
        srcs[k] = jnp.minimum(n0, DP - 1)
        srcs[16 + k] = jnp.minimum(n1, DP - 1)
        return carry

    lax.fori_loop(0, 16, source, 0)

    for d in range(1, TP):
        z = up(t - d, TP)
        links.landed(sqx.at[z], sq_base + d, (r, z))
    total = sqx[0]
    for z in range(1, TP):
        total = total + sqx[z]
    inv = lax.rsqrt(total / D + 1e-06)
    part1 = inv.astype(BF).astype(F32)
    part2 = (inv - part1).astype(BF).astype(F32)
    stack = jnp.concatenate([part1, part2, (inv - part1) - part2], axis=0)
    stack_t = stack.T.astype(BF)
    pick3 = jnp.concatenate([pick, pick, pick], axis=0).astype(BF)
    gains = gain[...]
    for i in range(4):
        scale = dot(stack_t[128 * i : 128 * i + 128], pick3, NN)
        v = pk[8 * i : 8 * i + 8].reshape(128, FEAT).astype(F32)
        nrm[8 * i : 8 * i + 8] = (v * scale * gains).astype(BF).reshape(8, ROWS, FEAT)

    def pack_rows(p, carry):
        sp[p] = nrm[up(p - mine_start + 1024, SLOTS)]
        return carry

    lax.fori_loop(0, DP, pack_rows, 0)
    row_base = links.take(CHIPS)
    exchange(sp, cp.at[c], row_base)

    @pl.when(jnp.logical_not(still))
    def _():
        links.landed(i2, relay_mid, plane(old_chip))
        links.landed(i1, relay_mid + 1, plane(old_chip))

    relay_along_z(lambda copy: copy.start())

    @pl.when(same)
    def _():
        w1f[Y, X] = i1[...]
        own = pltpu.make_async_copy(i2.at[c], relay_in(c), lsem)
        own.start()
        own.wait()

    exchanged(cp.at[c], row_base)
    row_sib = links.take(1)
    links.start(cp.at[c, :, 1 - c], cp.at[c, :, 1 - c], row_sib, sibling)

    cot_base = links.take(CHIPS)
    exchange(sc, cc.at[c], cot_base)

    links.landed(cp.at[1 - c, :, c], row_sib, sibling)

    def choose_rows(k, carry):
        s = srcs[16 * c + k]
        xf[t, 16 * c + k] = cp[lax.rem(s, 2), lax.div(s, 2), c]
        return carry

    lax.fori_loop(0, 16, choose_rows, 0)

    def ring_sum(part, rr, rl, base, s):
        br, bl = up(t + 4 - s, TP), up(t - 4 + s, TP)
        for u in range(2):
            k = base + 8 * u
            w = slice(256 * u, 256 * u + 256)
            if s == 0:
                links.start(part.at[br, 0:80, w], rr.at[0, 0:80, w], k, right)
                links.start(part.at[bl, 80:160, w], rl.at[0, 80:160, w], k + 4, left)
                continue
            lo, hi = (slice(0, 80), slice(80, 160)) if s == 1 else (slice(0, 160),) * 2
            links.landed(rr.at[s - 1, lo, w], k + s - 1, left)
            part[br, lo, w] = (part[br, lo, w].astype(F32) + rr[s - 1, lo, w].astype(F32)).astype(BF)
            links.start(part.at[br, :, w], rr.at[s, :, w], k + s, right)
            links.landed(rl.at[s - 1, hi, w], k + 4 + s - 1, right)
            part[bl, hi, w] = (part[bl, hi, w].astype(F32) + rl[s - 1, hi, w].astype(F32)).astype(BF)
            links.start(part.at[bl, :, w], rl.at[s, :, w], k + 4 + s, left)

    def ring_end(rr, rl, base, u):
        w = slice(256 * u, 256 * u + 256)
        links.landed(rr.at[3, :, w], base + 8 * u + 3, left)
        links.landed(rl.at[3, :, w], base + 8 * u + 7, right)

    def ring_copy(buf, base, s):
        br, bl = up(t - s, TP), up(t + s, TP)
        for u in range(2):
            k = base + 8 * u
            w = slice(256 * u, 256 * u + 256)
            if s > 0:
                links.landed(buf.at[br, :, w], k + s - 1, left)
            lo, hi = (slice(0, 160),) * 2 if s < 3 else (slice(0, 80), slice(80, 160))
            links.start(buf.at[br, lo, w], buf.at[br, lo, w], k + s, right)
            if s > 0:
                links.landed(buf.at[bl, :, w], k + 4 + s - 1, right)
            links.start(buf.at[bl, hi, w], buf.at[bl, hi, w], k + 4 + s, left)

    def ring_copied(buf, base):
        far = up(t + 4, TP)
        for u in range(2):
            w = slice(256 * u, 256 * u + 256)
            links.landed(buf.at[far, 0:80, w], base + 8 * u + 3, left)
            links.landed(buf.at[far, 80:160, w], base + 8 * u + 7, right)

    def around(s, work):
        def step(i, carry):
            work(up(t + (2 * i - 1) * s, TP))
            return carry

        lax.fori_loop(0, 2, step, 0)

    x_base = links.take(16)
    xs_base = links.take(18)

    def rows_of(z, u, start, size):
        return xf.at[z, pl.ds(16 * c + 8 * u + start, size)]

    def hand_over(z, u):
        ref = rows_of(z, u, 0, 8)
        links.start(ref, ref, xs_base + 2 * z + u, sibling)

    def handed(z):
        for u in range(2):
            links.landed(xf.at[z, pl.ds(16 * (1 - c) + 8 * u, 8)], xs_base + 2 * z + u, sibling)

    def ring_rows(s):
        br, bl = up(t - s, TP), up(t + s, TP)
        for u in range(2):
            k = x_base + 8 * u
            size = 8 if s < 3 else 4
            if s > 0:
                links.landed(rows_of(br, u, 0, 8), k + s - 1, left)
            ref = rows_of(br, u, 0, size)
            links.start(ref, ref, k + s, right)
            if s > 0:
                links.landed(rows_of(bl, u, 0, 8), k + 4 + s - 1, right)
            ref = rows_of(bl, u, 8 - size, size)
            links.start(ref, ref, k + 4 + s, left)
            hand_over(br, u)
            if s > 0:
                hand_over(bl, u)

    def ring_rows_end():
        far = up(t + 4, TP)
        for u in range(2):
            links.landed(rows_of(far, u, 0, 4), x_base + 8 * u + 3, left)
            ref = rows_of(far, u, 0, 4)
            links.start(ref, ref, xs_base + 2 * far + u, sibling)
            links.landed(rows_of(far, u, 4, 4), x_base + 8 * u + 7, right)
            ref = rows_of(far, u, 4, 4)
            links.start(ref, ref, xs_base + 16 + u, sibling)

    ring_rows(0)

    for e in range(2):

        @pl.when(jnp.logical_or(jnp.logical_not(same), e != c))
        def _(e=e):
            links.landed(relay_in(e), relay + e, sibling)

    gather_first(w2a, w2b, w2_base)

    @pl.when(jnp.logical_not(same))
    def _():
        links.landed(w1f.at[Y, X], relay1, (r, mate))

    gather_first(w1a, w1b, w1_base)

    def place(z):
        return lax.rem(z + t, TP)

    def grad_block(z):
        p = place(z)
        return dot(w2t[lax.div(p, 2), lax.rem(p, 2)], g[...].reshape(TOK, OUTW), NT)

    def grad_store(z):
        pg[z] = grad_block(z).astype(BF)

    def pre_add(z):
        p = place(z)
        rows = w1f[lax.div(p, 2), pl.ds(2 * lax.rem(p, 2), 2)].reshape(UNITS, FEAT)
        oh[...] += dot(rows, xf[z].reshape(TOK, FEAT), NT)

    pg_base = links.take(16)
    ht_base = links.take(16)
    def activate(u):
        w = slice(256 * u, 256 * u + 256)

        def step(i, carry):
            rows = pl.ds(pl.multiple_of(i * 32, 32), 32)
            v = oh[rows, w]
            cdf = 0.5 * (1.0 + lax.erf(v * 0.7071067811865476))
            density = jnp.exp(-0.5 * v * v) * 0.3989422804014327
            ht[t, rows, w] = (v * cdf).astype(BF)
            oh[rows, w] = cdf + v * density
            return carry

        lax.fori_loop(0, 5, step, 0)

    def descend(u):
        w = slice(256 * u, 256 * u + 256)

        def step(i, carry):
            rows = pl.ds(pl.multiple_of(i * 32, 32), 32)
            v = og[rows, w] + zgr[3, rows, w].astype(F32) + zgl[3, rows, w].astype(F32)
            gt[rows, w] = (v * oh[rows, w]).astype(BF)
            return carry

        lax.fori_loop(0, 5, step, 0)

    ring_rows(1)
    exchanged(cc.at[c], cot_base)
    cot_sib = links.take(1)
    links.start(cc.at[c], cc.at[c], cot_sib, sibling)

    gather_second(w2t.at[Y, :, 0:80], w2t.at[:, xh, 80:160, w2lane], w2_first, w2_base)

    gather_second(w1f.at[Y, :, 0:W1A], w1f.at[:, X, W1A:80], w1_first, w1_base)
    ring_rows(2)
    links.landed(cc.at[1 - c], cot_sib, sibling)

    def choose(j, carry):
        s = srcs[j]
        g[j] = cc[lax.rem(s, 2), lax.div(s, 2), lax.div(j, 16)]
        return carry

    lax.fori_loop(0, 32, choose, 0)

    for d in range(1, 4):
        xx, yy = up(X - d, 4), up(Y - d, 4)
        links.landed(w2t.at[yy, :, 0:80], w2_base + 6 + d, along_y(-d))
        links.landed(
            w2t.at[:, lax.div(xx, 2), 80:160, pl.ds(pl.multiple_of(lax.rem(xx, 2) * 256, 256), 256)],
            w2_base + 9 + d,
            along_x(-d),
        )

    grad_store(up(t + 4, TP))
    ring_sum(pg, zgr, zgl, pg_base, 0)
    around(3, grad_store)
    ring_rows(3)
    ring_sum(pg, zgr, zgl, pg_base, 1)
    around(2, grad_store)
    ring_sum(pg, zgr, zgl, pg_base, 2)
    around(1, grad_store)
    og[...] = grad_block(t)
    for d in range(1, 4):
        xx, yy = up(X - d, 4), up(Y - d, 4)
        links.landed(w1f.at[yy, :, 0:W1A], w1_base + 6 + d, along_y(-d))
        links.landed(w1f.at[:, xx, W1A:80], w1_base + 9 + d, along_x(-d))
    oh[...] = jnp.concatenate([b1[c]] * 4, axis=1)
    handed(t)
    pre_add(t)
    for s in range(1, 3):
        handed(up(t - s, TP))
        handed(up(t + s, TP))
        around(s, pre_add)
    ring_rows_end()
    handed(up(t - 3, TP))
    handed(up(t + 3, TP))
    around(3, pre_add)
    ring_sum(pg, zgr, zgl, pg_base, 3)
    far_rows = xf.at[up(t + 4, TP)]
    for u in range(2):
        for i in range(2):
            ref = far_rows.at[pl.ds(16 * (1 - c) + 8 * u + 4 * i, 4)]
            links.landed(ref, xs_base + (2 * up(t + 4, TP) if i == 0 else 16) + u, sibling)
    pre_add(up(t + 4, TP))

    for u in range(2):
        activate(u)
    ring_copy(ht, ht_base, 0)
    def plane_send(part, cut, ra, rb, base, z):
        yy, par = lax.div(z, 2), lax.rem(z, 2)
        dy = up(yy - Y, 4)

        @pl.when(dy != 0)
        def _():
            links.make(
                part.at[yy, pl.ds(2 * par, 2), 0:cut],
                ra.at[dy - 1, pl.ds(2 * par, 2)],
                base + 2 * (dy - 1) + par,
                along_y(dy),
            ).start()

        for i in range(2):
            xx = 2 * par + i
            dx = up(xx - X, 4)

            @pl.when(dx != 0)
            def _(xx=xx, dx=dx):
                links.make(
                    part.at[yy, xx, cut:],
                    rb.at[dx - 1, yy],
                    base + 6 + 4 * (dx - 1) + yy,
                    along_x(dx),
                ).start()

    def plane_sent(part, cut, ra, rb, sa, sbx, rc, rd, base):
        def waits():
            for d in range(3):
                for i in range(2):
                    links.make(part.at[0, 0:2, 0:cut], ra.at[d, 0:2], base + 2 * d + i, along_y(1)).wait_send()
                for i in range(4):
                    links.make(part.at[0, 0, cut:], rb.at[d, 0], base + 6 + 4 * d + i, along_x(1)).wait_send()
                links.make(sa.at[0], rc.at[d], base + 19 + d, along_x(1)).wait_send()
                links.make(sbx.at[0], rd.at[d], base + 22 + d, along_y(1)).wait_send()

        links.open.append(waits)

    def plane_second(part, cut, ra, rb, sa, sbx, rc, rd, base, z):
        p = place(z)
        yy, par = lax.div(p, 2), lax.rem(p, 2)

        @pl.when(Y == yy)
        def _():
            for d in range(3):
                links.landed(ra.at[d, pl.ds(2 * par, 2)], base + 2 * d + par, along_y(-d - 1))
            for i in range(2):
                xx = 2 * par + i
                v = part[yy, xx, 0:cut].astype(F32)
                for d in range(3):
                    v = v + ra[d, xx].astype(F32)
                sa[xx] = v.astype(BF)
                dx = up(xx - X, 4)

                @pl.when(dx != 0)
                def _(xx=xx, dx=dx):
                    links.make(sa.at[xx], rc.at[dx - 1], base + 18 + dx, along_x(dx)).start()

        @pl.when(lax.div(X, 2) == par)
        def _():
            for d in range(3):
                links.landed(rb.at[d, yy], base + 6 + 4 * d + yy, along_x(-d - 1))
            v = part[yy, X, cut:].astype(F32)
            for d in range(3):
                v = v + rb[d, yy].astype(F32)
            sbx[yy] = v.astype(BF)
            dy = up(yy - Y, 4)

            @pl.when(dy != 0)
            def _():
                links.make(sbx.at[yy], rd.at[dy - 1], base + 21 + dy, along_y(dy)).start()

    def plane_sum_end(sa, sbx, rc, rd, base):
        for d in range(1, 4):
            links.landed(rc.at[d - 1], base + 18 + d, along_x(-d))
        va = sa[X].astype(F32)
        for d in range(3):
            va = va + rc[d].astype(F32)
        for d in range(1, 4):
            links.landed(rd.at[d - 1], base + 21 + d, along_y(-d))
        vb = sbx[Y].astype(F32)
        for d in range(3):
            vb = vb + rd[d].astype(F32)
        return va.astype(BF), vb.astype(BF)

    g2_base = links.take(25)

    def second_grad(z):
        p = place(z)
        v = dot(ht[z], g[...].reshape(TOK, OUTW), NN).astype(BF)
        for i in range(2):
            g2[lax.div(p, 2), 2 * lax.rem(p, 2) + i] = v[:, 256 * i : 256 * i + 256]
        plane_send(g2, 80, a2, c2, g2_base, p)

    def second_second(z):
        plane_second(g2, 80, a2, c2, s2a, s2b, d2, e2, g2_base, z)

    def embed(z):
        p = place(z)

        def step(i, carry):
            lanes = pl.ds(pl.multiple_of(i * 128, 128), 128)
            rows = ht[z, :, lanes].astype(F32).T.astype(BF)
            v = dot(rows, w2t[lax.div(p, 2), lax.rem(p, 2)], NN)
            pe[pl.ds(8 * i, 8)] += v.reshape(8, ROWS, OUTW)
            return carry

        lax.fori_loop(0, 4, step, 0)

    def use_hidden(z):
        second_grad(z)
        embed(z)

    plane_sent(g2, 80, a2, c2, s2a, s2b, d2, e2, g2_base)

    g1_base = links.take(25)

    def first_grad(z):
        p = place(z)
        v = dot(gt[...], xf[z].reshape(TOK, FEAT), NN).astype(BF)
        for i in range(2):
            g1[lax.div(p, 2), 2 * lax.rem(p, 2) + i] = v[80 * i : 80 * i + 80]
        plane_send(g1, W1A, a1, c1, g1_base, p)

    plane_sent(g1, W1A, a1, c1, s1a, s1b, d1, e1, g1_base)
    def first_second(z):
        plane_second(g1, W1A, a1, c1, s1a, s1b, d1, e1, g1_base, z)

    for u in range(2):
        ring_end(zgr, zgl, pg_base, u)
        descend(u)

    lax.fori_loop(0, TP, lambda z, carry: (first_grad(z), carry)[1], 0)
    pe[...] = jnp.zeros_like(pe)
    use_hidden(t)
    ring_copy(ht, ht_base, 1)
    around(1, use_hidden)
    ring_copy(ht, ht_base, 2)
    around(2, use_hidden)
    ring_copy(ht, ht_base, 3)
    lax.fori_loop(0, TP, lambda z, carry: (first_second(z), carry)[1], 0)

    around(3, use_hidden)
    second_second(t)
    around(1, second_second)
    va, vb = plane_sum_end(s1a, s1b, d1, e1, g1_base)
    t1[0:W1A] = va
    t1[W1A:80] = vb
    back1 = links.take(2)

    def back1_z(do):
        @pl.when(jnp.logical_not(same))
        def _():
            do(links.make(t1, k1, back1, (r, mate)))

    back1_z(lambda copy: copy.start())

    @pl.when(same)
    def _():
        k1[...] = t1[...]

    links.open.append(lambda: back1_z(lambda copy: copy.wait_send()))

    ring_copied(ht, ht_base)
    use_hidden(up(t + 4, TP))

    def window_of(s, e):
        first = starts[s]
        slot = lax.rem(2 * m + e - first + 1024, SLOTS)
        return e * 16 + jnp.minimum(lax.div(first + slot, 32), 15)

    def pack_sibling(i, carry):
        for e in range(2):
            ps[2 * i + e] = pe[window_of(2 * i + 1 - c, e)].astype(BF)
        return carry

    lax.fori_loop(0, CHIPS, pack_sibling, 0)
    emb_sib = links.take(1)
    links.start(ps, pr, emb_sib, sibling)

    around(2, second_second)
    @pl.when(jnp.logical_not(same))
    def _():
        links.landed(k1, back1, (r, mate))

    def back1_plane(do):
        @pl.when(jnp.logical_not(still))
        def _():
            do(links.make(k1, gw1, back1 + 1, plane(old_chip)))

    back1_plane(lambda copy: copy.start())

    @pl.when(still)
    def _():
        gw1[...] = k1[...]

    links.open.append(lambda: back1_plane(lambda copy: copy.wait_send()))

    links.landed(pr, emb_sib, sibling)
    bias2 = b2[...]

    def pack_home(i, carry):
        for e in range(2):
            v = pe[window_of(2 * i + c, e)] + pr[2 * i + e].astype(F32) + bias2
            sb[2 * i + e] = v.astype(BF)
        return carry

    lax.fori_loop(0, CHIPS, pack_home, 0)
    home_base = links.take(CHIPS)
    exchange(sb, bk, home_base)

    around(3, second_second)
    second_second(up(t + 4, TP))
    va, vb = plane_sum_end(s2a, s2b, d2, e2, g2_base)
    for e in range(2):
        t2[e, 0:80] = va[:, 128 * e : 128 * e + 128]
        t2[e, 80:160] = vb[:, 128 * e : 128 * e + 128]
    back = links.take(3)

    def back_z(do):
        @pl.when(jnp.logical_not(same))
        def _():
            for e in range(2):
                do(links.make(t2.at[e], k2.at[c], back + c, (2 * m + e, mate), back + e))

        @pl.when(same)
        def _():
            do(links.make(t2.at[1 - c], k2.at[c], back + c, sibling, back + 1 - c))

    back_z(lambda copy: copy.start())

    @pl.when(same)
    def _():
        k2[c] = t2[c]

    links.open.append(lambda: back_z(lambda copy: copy.wait_send()))

    for e in range(2):

        @pl.when(jnp.logical_or(jnp.logical_not(same), e != c))
        def _(e=e):
            links.landed(k2.at[e], back + e, (2 * m + e, mate))

    def back_plane(do):
        @pl.when(jnp.logical_not(still))
        def _():
            do(links.make(k2, gw2, back + 2, plane(old_chip)))

    back_plane(lambda copy: copy.start())

    @pl.when(still)
    def _():
        gw2[...] = k2[...]

    links.open.append(lambda: back_plane(lambda copy: copy.wait_send()))

    exchanged(bk, home_base)

    def home(j, carry):
        p = lax.rem(mine_start + j, DP)
        v = bk[lax.div(p, 2), lax.rem(p, 2)].astype(F32)
        emb[j] = jnp.where(j < mine_count, v, 0.0).astype(BF)
        return carry

    lax.fori_loop(0, SLOTS, home, 0)

    @pl.when(jnp.logical_not(still))
    def _():
        links.landed(gw1, back1 + 1, plane(mid_chip))
        links.landed(gw2, back + 2, plane(mid_chip))

    links.finish()


def on_device(patches, norm_gain, w_first, b_first, w_second, b_second, counts, cotangent):
    pk = patches.reshape(SLOTS, ROWS, FEAT)
    w1 = w_first.reshape(80, FEAT)
    w2p = w_second.T.reshape(2, 2, 80, 128).transpose(1, 0, 2, 3).reshape(2, UNITS, 128)
    b1 = b_first.astype(F32).reshape(2, 2, 80).transpose(1, 0, 2).reshape(2, UNITS, 1)
    b1 = jnp.broadcast_to(b1, (2, UNITS, 128))
    b2 = b_second.astype(F32).reshape(1, OUTW)
    gain = jnp.tile(norm_gain.astype(F32).reshape(1, 160), (1, 4))
    cot = cotangent.reshape(SLOTS, ROWS, OUTW)

    vmem = pl.BlockSpec(memory_space=pltpu.VMEM)
    V = pltpu.VMEM
    S = pltpu.SMEM
    emb, gw1, gw2 = pl.pallas_call(
        kernel,
        name="merger",
        out_shape=(
            jax.ShapeDtypeStruct((SLOTS, ROWS, OUTW), BF),
            jax.ShapeDtypeStruct((80, FEAT), BF),
            jax.ShapeDtypeStruct((2, UNITS, 128), BF),
        ),
        in_specs=[pl.BlockSpec(memory_space=pltpu.SMEM)] + [vmem] * 7,
        out_specs=(vmem, vmem, vmem),
        scratch_shapes=[
            pltpu.SemaphoreType.DMA((256,)),
            pltpu.SemaphoreType.DMA((256,)),
            pltpu.SemaphoreType.DMA,
            S((DP,), jnp.int32),
            S((DP,), jnp.int32),
            S((DP,), jnp.int32),
            V((DP, ROWS, OUTW), BF),
            V((2, CHIPS, 2, ROWS, OUTW), BF),
            V((32, ROWS, OUTW), BF),
            V((SLOTS, ROWS, FEAT), BF),
            V((DP, ROWS, FEAT), BF),
            V((2, CHIPS, 2, ROWS, FEAT), BF),
            V((TP, 32, ROWS, FEAT), BF),
            V((TP, 8, TOK), F32),
            V((4, 4, 80, FEAT), BF),
            V((4, 2, UNITS, OUTW), BF),
            V((TP, UNITS, TOK), BF),
            V((4, UNITS, TOK), BF),
            V((4, UNITS, TOK), BF),
            V((UNITS, TOK), F32),
            V((UNITS, TOK), F32),
            V((TP, UNITS, TOK), BF),
            V((UNITS, TOK), BF),
            V((32, ROWS, OUTW), F32),
            V((32, ROWS, OUTW), BF),
            V((32, ROWS, OUTW), BF),
            V((32, ROWS, OUTW), BF),
            V((CHIPS, 2, ROWS, OUTW), BF),
            V((4, 4, UNITS, 256), BF),
            V((3, 4, 80, 256), BF),
            V((3, 4, 80, 256), BF),
            V((4, 80, 256), BF),
            V((4, 80, 256), BF),
            V((3, 80, 256), BF),
            V((3, 80, 256), BF),
            V((2, UNITS, 128), BF),
            V((4, 4, 80, FEAT), BF),
            V((3, 4, W1A, FEAT), BF),
            V((3, 4, 80 - W1A, FEAT), BF),
            V((4, W1A, FEAT), BF),
            V((4, 80 - W1A, FEAT), BF),
            V((3, W1A, FEAT), BF),
            V((3, 80 - W1A, FEAT), BF),
            V((80, FEAT), BF),
            V((80, FEAT), BF),
            V((2, UNITS, 128), BF),
            V((80, FEAT), BF),
            V((2, UNITS, 128), BF),
        ],
        compiler_params=pltpu.CompilerParams(
            collective_id=0, has_side_effects=True, vmem_limit_bytes=56 * 1024 * 1024
        ),
        cost_estimate=pl.CostEstimate(
            flops=3_700_000_000, bytes_accessed=3_000_000, transcendentals=200_000
        ),
    )(counts, pk, w1, w2p, b1, b2, gain, cot)
    embeddings = emb.reshape(SLOTS * ROWS, OUTW)
    grad_w1 = gw1.reshape(80, 4, 160)
    grad_w2 = gw2.reshape(2, 2, 80, 128).transpose(3, 1, 0, 2).reshape(128, 320)
    return embeddings, grad_w1, grad_w2


def solution(mesh):
    in_specs = (
        P("dp", "tensor"),
        P("tensor"),
        P("dp", None, "tensor"),
        P("tensor"),
        P("dp", "tensor"),
        P("tensor"),
        P(),
        P("dp", "tensor"),
    )
    out_specs = (P("dp", "tensor"), P("dp", None, "tensor"), P("dp", "tensor"))
    return jax.shard_map(
        on_device, mesh=mesh, in_specs=in_specs, out_specs=out_specs, check_vma=False
    )
```

time: 163 us -> 137 us (0.84)
  the two profiles are of different devices: /device:TPU:6 before, /device:TPU:56 now
where the time goes in v2:
time: 137 us; the launch traced here: 136 us
  Pallas kernels  123 us (90%)
  local copies, waits for them, and re-layouts  11.8 us (9%)
    pallas_call x1, Pallas kernels, on_device(): pl.pallas_call(kernel, name='merger', out_shape=(jax.ShapeDtypeStruct((SL...  123 us
    unnamed x14, local copies, waits for them, and re-layouts  4.06 us

profile of v2, /device:TPU:56, one launch (start us, length us, event | category | flops | bytes accessed | tf_op | source)
XLA Modules:
  0.0 136.5 jit_solution(12816418542173558435)
XLA Ops:
  0.6 1.4 %copy.17 = bf16[2048,160]{1,0:T(8,128)(2,1)S(1)} copy(bf16[2048,160]{0,1:T(8,128)(2,1)} %param.8) | data formatting | bytes 1310720 | tf_op args[0]
  2.0 0.0 copy-start.3
  2.1 2.3 %reshape.50.pk = bf16[32,16,640]{2,1,0:T(8,128)(2,1)} reshape(bf16[2048,160]{1,0:T(8,128)(2,1)S(1)} %copy.17) | data formatting | bytes 1310720 | tf_op jit(solution)/shard_map/reshape | solution.py:801
  4.4 0.0 copy-done.3
  4.4 0.0 copy-start
  4.4 0.1 reshape.65
  4.5 0.1 reshape.62
  4.6 0.8 broadcast_in_dim.12.b1
  5.4 0.0 copy-done
  5.4 0.0 copy-start.1
  5.4 0.8 reshape.51.w1
  6.2 0.1 copy-done.1
  6.3 0.6 copy.18
  6.9 0.0 copy-start.5
  6.9 0.7 copy-done.5
  7.6 0.0 copy-start.4
  7.6 0.7 tile.9.gain
  8.2 0.0 copy-done.4
  8.2 0.6 reshape.63
  8.8 123.4 %merger.1 = (bf16[32,16,512]{2,1,0:T(8,128)(2,1)}, bf16[80,640]{1,0:T(8,128)(2,1)}, bf16[2,160,128]{2,1,0:T(8,128)(2,1)}) custom-call(s32[32]{0:T(128)} %counts.1, bf16[32,16,640]{2,1,0:T(8,128)(2,1)} %reshape.50.pk, bf16[80,640]{1,0:T(8,128)(2,1)} %reshape.51.w1, bf16[2,160,128]{2,1,0:T(8,128)(2,1)} %bitcast.17, f32[2,160,128]{2,1,0:T(8,128)} %broadcast_in_dim.12.b1, ...), custom_call_target="tpu_custom_call" | custom-call | flops 3700000000 | bytes 3000000 | tf_op jit(solution)/shard_map/merger/pallas_call | solution.py:813
  132.2 0.0 copy-start.2
  132.2 1.8 %reshape.59 = bf16[80,4,160]{2,1,0:T(4,128)(2,1)} reshape(bf16[80,640]{1,0:T(8,128)(2,1)} %get-tuple-element.7) | data formatting | bytes 204800 | tf_op jit(solution)/shard_map/reshape | solution.py:881
  134.0 0.0 copy-done.2
  134.0 0.6 copy.20
  134.6 1.9 %copy.22 = bf16[512,512]{1,0:T(8,128)(2,1)} copy(bf16[512,512]{1,0:T(8,128)(2,1)} %bitcast.14) | data formatting | bytes 1048576
  (2 shorter events, 0.0 us)
Async XLA Ops:
  2.0 2.4 %copy-start.3 = (bf16[320]{0:T(512)(128)(2,1)S(1)}, bf16[320]{0:T(512)(128)(2,1)}, u32[]{:S(2)}) copy-start(bf16[320]{0:T(512)(128)(2,1)} %param.11) | copy-start | bytes 1924
  4.4 1.0 copy-start
  5.4 0.9 copy-start.1
  6.9 0.7 copy-start.5
  7.6 0.7 copy-start.4
  132.2 1.8 %copy-start.2 = (bf16[2,160,128]{2,1,0:T(8,128)(2,1)S(1)}, bf16[2,160,128]{2,1,0:T(8,128)(2,1)}, u32[]{:S(2)}) copy-start(bf16[2,160,128]{2,1,0:T(8,128)(2,1)} %get-tuple-element.8) | copy-start | bytes 245764

commit v3 on v2

--- a/solution.py
+++ b/solution.py
@@ -72,7 +72,7 @@
 
 
 def kernel(
-    counts, pk, w1, w2p, b1, b2, gain, cot,
+    counts, patches_t, w1, w2p, b1, b2, gain, cot,
     emb, gw1, gw2,
     send, recv, lsem, starts, ends, srcs,
     sc, cc, g, nrm, sp, cp, xf, sqx,
@@ -82,7 +82,7 @@
     pe, ps, pr, sb, bk,
     g2, a2, c2, s2a, s2b, d2, e2, t2,
     g1, a1, c1, s1a, s1b, d1, e1, t1,
-    i1, i2, k1, k2,
+    i1, i2, k1, k2, b1s, pk,
 ):
     r = lax.axis_index("dp")
     t = lax.axis_index("tensor")
@@ -141,12 +141,23 @@
     lead = jnp.logical_and(lane >= row * 160, lane < row * 160 + 160)
     pick = jnp.where(lead, 1.0, 0.0).astype(F32)
     pick_bf = pick.astype(BF)
+    line = lax.broadcasted_iota(jnp.int32, (256, 256), 0)
+    col = lax.broadcasted_iota(jnp.int32, (256, 256), 1)
+    order = jnp.where(col == 4 * lax.rem(line, 64) + lax.div(line, 64), 1.0, 0.0).astype(BF)
     for i in range(4):
-        v = pk[8 * i : 8 * i + 8].reshape(128, FEAT).astype(F32)
+        halves = []
+        for j in range(2):
+            at = 512 * i + 256 * j
+            v = dot(order, patches_t[:, at : at + 256], NT)
+            halves.append(jnp.concatenate([v[64 * p : 64 * p + 64] for p in range(4)], axis=1))
+        v = jnp.concatenate(halves, axis=0)
+        pk[8 * i : 8 * i + 8] = v.astype(BF).reshape(8, ROWS, FEAT)
         sq = v * v
         high = sq.astype(BF)
         low = (sq - high.astype(F32)).astype(BF)
         sqx[t, :, 128 * i : 128 * i + 128] = dot(pick_bf, high, NT) + dot(pick_bf, low, NT)
+    gains = jnp.concatenate([gain[...].astype(F32).reshape(1, 160)] * 4, axis=1)
+    b1s[...] = jnp.broadcast_to(b1[...].astype(F32).reshape(1, 320), (128, 320)).T.reshape(2, 2, 80, 128)
 
     pl.semaphore_wait(barrier, 23 + jnp.where(same, 0, 1))
 
@@ -269,7 +280,6 @@
     stack = jnp.concatenate([part1, part2, (inv - part1) - part2], axis=0)
     stack_t = stack.T.astype(BF)
     pick3 = jnp.concatenate([pick, pick, pick], axis=0).astype(BF)
-    gains = gain[...]
     for i in range(4):
         scale = dot(stack_t[128 * i : 128 * i + 128], pick3, NN)
         v = pk[8 * i : 8 * i + 8].reshape(128, FEAT).astype(F32)
@@ -296,6 +306,14 @@
         own = pltpu.make_async_copy(i2.at[c], relay_in(c), lsem)
         own.start()
         own.wait()
+
+    for e in range(2):
+
+        @pl.when(jnp.logical_or(jnp.logical_not(same), e != c))
+        def _(e=e):
+            links.landed(relay_in(e), relay + e, sibling)
+
+    gather_first(w2a, w2b, w2_base)
 
     exchanged(cp.at[c], row_base)
     row_sib = links.take(1)
@@ -405,13 +423,7 @@
 
     ring_rows(0)
 
-    for e in range(2):
-
-        @pl.when(jnp.logical_or(jnp.logical_not(same), e != c))
-        def _(e=e):
-            links.landed(relay_in(e), relay + e, sibling)
-
-    gather_first(w2a, w2b, w2_base)
+    gather_second(w2t.at[Y, :, 0:80], w2t.at[:, xh, 80:160, w2lane], w2_first, w2_base)
 
     @pl.when(jnp.logical_not(same))
     def _():
@@ -461,15 +473,11 @@
 
         lax.fori_loop(0, 5, step, 0)
 
-    ring_rows(1)
     exchanged(cc.at[c], cot_base)
     cot_sib = links.take(1)
     links.start(cc.at[c], cc.at[c], cot_sib, sibling)
 
-    gather_second(w2t.at[Y, :, 0:80], w2t.at[:, xh, 80:160, w2lane], w2_first, w2_base)
-
-    gather_second(w1f.at[Y, :, 0:W1A], w1f.at[:, X, W1A:80], w1_first, w1_base)
-    ring_rows(2)
+    ring_rows(1)
     links.landed(cc.at[1 - c], cot_sib, sibling)
 
     def choose(j, carry):
@@ -491,9 +499,11 @@
     grad_store(up(t + 4, TP))
     ring_sum(pg, zgr, zgl, pg_base, 0)
     around(3, grad_store)
-    ring_rows(3)
+    gather_second(w1f.at[Y, :, 0:W1A], w1f.at[:, X, W1A:80], w1_first, w1_base)
+    ring_rows(2)
     ring_sum(pg, zgr, zgl, pg_base, 1)
     around(2, grad_store)
+    ring_rows(3)
     ring_sum(pg, zgr, zgl, pg_base, 2)
     around(1, grad_store)
     og[...] = grad_block(t)
@@ -501,18 +511,18 @@
         xx, yy = up(X - d, 4), up(Y - d, 4)
         links.landed(w1f.at[yy, :, 0:W1A], w1_base + 6 + d, along_y(-d))
         links.landed(w1f.at[:, xx, W1A:80], w1_base + 9 + d, along_x(-d))
-    oh[...] = jnp.concatenate([b1[c]] * 4, axis=1)
+    oh[...] = jnp.concatenate([b1s[:, c].reshape(UNITS, 128)] * 4, axis=1)
     handed(t)
     pre_add(t)
     for s in range(1, 3):
         handed(up(t - s, TP))
         handed(up(t + s, TP))
         around(s, pre_add)
+    ring_sum(pg, zgr, zgl, pg_base, 3)
     ring_rows_end()
     handed(up(t - 3, TP))
     handed(up(t + 3, TP))
     around(3, pre_add)
-    ring_sum(pg, zgr, zgl, pg_base, 3)
     far_rows = xf.at[up(t + 4, TP)]
     for u in range(2):
         for i in range(2):
@@ -663,11 +673,31 @@
     ring_copy(ht, ht_base, 2)
     around(2, use_hidden)
     ring_copy(ht, ht_base, 3)
+    around(3, use_hidden)
     lax.fori_loop(0, TP, lambda z, carry: (first_second(z), carry)[1], 0)
 
-    around(3, use_hidden)
+    ring_copied(ht, ht_base)
+    use_hidden(up(t + 4, TP))
+
+    def window_of(s, e):
+        first = starts[s]
+        slot = lax.rem(2 * m + e - first + 1024, SLOTS)
+        return e * 16 + jnp.minimum(lax.div(first + slot, 32), 15)
+
+    def pack_sibling(i, carry):
+        for e in range(2):
+            ps[2 * i + e] = pe[window_of(2 * i + 1 - c, e)].astype(BF)
+        return carry
+
+    lax.fori_loop(0, CHIPS, pack_sibling, 0)
+    emb_sib = links.take(1)
+    links.start(ps, pr, emb_sib, sibling)
+
     second_second(t)
     around(1, second_second)
+    around(2, second_second)
+    around(3, second_second)
+    second_second(up(t + 4, TP))
     va, vb = plane_sum_end(s1a, s1b, d1, e1, g1_base)
     t1[0:W1A] = va
     t1[W1A:80] = vb
@@ -686,43 +716,32 @@
 
     links.open.append(lambda: back1_z(lambda copy: copy.wait_send()))
 
-    ring_copied(ht, ht_base)
-    use_hidden(up(t + 4, TP))
-
-    def window_of(s, e):
-        first = starts[s]
-        slot = lax.rem(2 * m + e - first + 1024, SLOTS)
-        return e * 16 + jnp.minimum(lax.div(first + slot, 32), 15)
-
-    def pack_sibling(i, carry):
-        for e in range(2):
-            ps[2 * i + e] = pe[window_of(2 * i + 1 - c, e)].astype(BF)
-        return carry
-
-    lax.fori_loop(0, CHIPS, pack_sibling, 0)
-    emb_sib = links.take(1)
-    links.start(ps, pr, emb_sib, sibling)
-
-    around(2, second_second)
-    @pl.when(jnp.logical_not(same))
-    def _():
-        links.landed(k1, back1, (r, mate))
-
-    def back1_plane(do):
-        @pl.when(jnp.logical_not(still))
-        def _():
-            do(links.make(k1, gw1, back1 + 1, plane(old_chip)))
-
-    back1_plane(lambda copy: copy.start())
-
-    @pl.when(still)
-    def _():
-        gw1[...] = k1[...]
-
-    links.open.append(lambda: back1_plane(lambda copy: copy.wait_send()))
+    va, vb = plane_sum_end(s2a, s2b, d2, e2, g2_base)
+    for e in range(2):
+        t2[e, 0:80] = va[:, 128 * e : 128 * e + 128]
+        t2[e, 80:160] = vb[:, 128 * e : 128 * e + 128]
+    back = links.take(3)
+
+    def back_z(do):
+        @pl.when(jnp.logical_not(same))
+        def _():
+            for e in range(2):
+                do(links.make(t2.at[e], k2.at[c], back + c, (2 * m + e, mate), back + e))
+
+        @pl.when(same)
+        def _():
+            do(links.make(t2.at[1 - c], k2.at[c], back + c, sibling, back + 1 - c))
+
+    back_z(lambda copy: copy.start())
+
+    @pl.when(same)
+    def _():
+        k2[c] = t2[c]
+
+    links.open.append(lambda: back_z(lambda copy: copy.wait_send()))
 
     links.landed(pr, emb_sib, sibling)
-    bias2 = b2[...]
+    bias2 = b2[...].astype(F32).reshape(1, OUTW)
 
     def pack_home(i, carry):
         for e in range(2):
@@ -734,31 +753,22 @@
     home_base = links.take(CHIPS)
     exchange(sb, bk, home_base)
 
-    around(3, second_second)
-    second_second(up(t + 4, TP))
-    va, vb = plane_sum_end(s2a, s2b, d2, e2, g2_base)
-    for e in range(2):
-        t2[e, 0:80] = va[:, 128 * e : 128 * e + 128]
-        t2[e, 80:160] = vb[:, 128 * e : 128 * e + 128]
-    back = links.take(3)
-
-    def back_z(do):
-        @pl.when(jnp.logical_not(same))
-        def _():
-            for e in range(2):
-                do(links.make(t2.at[e], k2.at[c], back + c, (2 * m + e, mate), back + e))
-
-        @pl.when(same)
-        def _():
-            do(links.make(t2.at[1 - c], k2.at[c], back + c, sibling, back + 1 - c))
-
-    back_z(lambda copy: copy.start())
-
-    @pl.when(same)
-    def _():
-        k2[c] = t2[c]
-
-    links.open.append(lambda: back_z(lambda copy: copy.wait_send()))
+    @pl.when(jnp.logical_not(same))
+    def _():
+        links.landed(k1, back1, (r, mate))
+
+    def back1_plane(do):
+        @pl.when(jnp.logical_not(still))
+        def _():
+            do(links.make(k1, gw1, back1 + 1, plane(old_chip)))
+
+    back1_plane(lambda copy: copy.start())
+
+    @pl.when(still)
+    def _():
+        gw1[...] = k1[...]
+
+    links.open.append(lambda: back1_plane(lambda copy: copy.wait_send()))
 
     for e in range(2):
 
@@ -798,13 +808,9 @@
 
 
 def on_device(patches, norm_gain, w_first, b_first, w_second, b_second, counts, cotangent):
-    pk = patches.reshape(SLOTS, ROWS, FEAT)
+    patches_t = patches.T
     w1 = w_first.reshape(80, FEAT)
     w2p = w_second.T.reshape(2, 2, 80, 128).transpose(1, 0, 2, 3).reshape(2, UNITS, 128)
-    b1 = b_first.astype(F32).reshape(2, 2, 80).transpose(1, 0, 2).reshape(2, UNITS, 1)
-    b1 = jnp.broadcast_to(b1, (2, UNITS, 128))
-    b2 = b_second.astype(F32).reshape(1, OUTW)
-    gain = jnp.tile(norm_gain.astype(F32).reshape(1, 160), (1, 4))
     cot = cotangent.reshape(SLOTS, ROWS, OUTW)
 
     vmem = pl.BlockSpec(memory_space=pltpu.VMEM)
@@ -869,6 +875,8 @@
             V((2, UNITS, 128), BF),
             V((80, FEAT), BF),
             V((2, UNITS, 128), BF),
+            V((2, 2, 80, 128), F32),
+            V((SLOTS, ROWS, FEAT), BF),
         ],
         compiler_params=pltpu.CompilerParams(
             collective_id=0, has_side_effects=True, vmem_limit_bytes=56 * 1024 * 1024
@@ -876,7 +884,7 @@
         cost_estimate=pl.CostEstimate(
             flops=3_700_000_000, bytes_accessed=3_000_000, transcendentals=200_000
         ),
-    )(counts, pk, w1, w2p, b1, b2, gain, cot)
+    )(counts, patches_t, w1, w2p, b_first, b_second, norm_gain, cot)
     embeddings = emb.reshape(SLOTS * ROWS, OUTW)
     grad_w1 = gw1.reshape(80, 4, 160)
     grad_w2 = gw2.reshape(2, 2, 80, 128).transpose(3, 1, 0, 2).reshape(128, 320)

time: 137 us -> 122 us (0.89)
  the two profiles are of different devices: /device:TPU:56 before, /device:TPU:164 now
where the time goes in v3:
time: 122 us; the launch traced here: 121 us
  Pallas kernels  114 us (93%)
  local copies, waits for them, and re-layouts  6.62 us (5%)
    pallas_call x1, Pallas kernels, on_device(): pl.pallas_call(kernel, name='merger', out_shape=(jax.ShapeDtypeStruct((SL...  114 us

profile of v3, /device:TPU:164, one launch (start us, length us, event | category | flops | bytes accessed | tf_op | source)
XLA Modules:
  0.0 121.3 jit_solution(3565116511351355058)
XLA Ops:
  0.6 0.0 copy-start
  0.6 1.6 %copy.11 = bf16[2,2,80,128]{3,2,0,1:T(8,128)(2,1)} copy(bf16[2,2,80,128]{3,2,1,0:T(8,128)(2,1)} %bitcast.14) | data formatting | bytes 163840 | tf_op jit(solution)/shard_map/reshape | solution.py:813
  2.2 0.0 copy-done
  2.2 0.8 reshape.30.w1
  3.0 114.0 %merger.1 = (bf16[32,16,512]{2,1,0:T(8,128)(2,1)}, bf16[80,640]{1,0:T(8,128)(2,1)}, bf16[2,160,128]{2,1,0:T(8,128)(2,1)}) custom-call(s32[32]{0:T(128)} %counts.1, bf16[160,2048]{1,0:T(8,128)(2,1)} %bitcast.18, bf16[80,640]{1,0:T(8,128)(2,1)} %reshape.30.w1, bf16[2,160,128]{2,1,0:T(8,128)(2,1)} %bitcast.17, bf16[320]{0:T(512)(128)(2,1)} %b1.1, ...), custom_call_target="tpu_custom_call" | custom-call | flops 3700000000 | bytes 3000000 | tf_op jit(solution)/shard_map/merger/pallas_call | solution.py:819
  117.0 0.0 copy-start.1
  117.0 1.6 %copy.12 = bf16[128,2,2,80]{0,3,2,1:T(8,128)(2,1)} copy(bf16[128,2,2,80]{0,3,1,2:T(8,128)(2,1)} %bitcast.16) | data formatting | bytes 163840 | tf_op jit(solution)/shard_map/transpose | solution.py:890
  118.6 0.0 copy-done.1
  118.6 0.8 reshape.35
  119.4 1.9 %copy.14 = bf16[512,512]{1,0:T(8,128)(2,1)} copy(bf16[512,512]{1,0:T(8,128)(2,1)} %bitcast.13) | data formatting | bytes 1048576
Async XLA Ops:
  0.6 1.6 %copy-start = (bf16[80,4,160]{2,1,0:T(4,128)(2,1)S(1)}, bf16[80,4,160]{2,1,0:T(4,128)(2,1)}, u32[]{:S(2)}) copy-start(bf16[80,4,160]{2,1,0:T(4,128)(2,1)} %param.10) | copy-start | bytes 307204
  117.0 1.6 %copy-start.1 = (bf16[80,640]{1,0:T(8,128)(2,1)S(1)}, bf16[80,640]{1,0:T(8,128)(2,1)}, u32[]{:S(2)}) copy-start(bf16[80,640]{1,0:T(8,128)(2,1)} %get-tuple-element.7) | copy-start | bytes 307204

commit v4 on v3

--- a/solution.py
+++ b/solution.py
@@ -72,7 +72,7 @@
 
 
 def kernel(
-    counts, patches_t, w1, w2p, b1, b2, gain, cot,
+    counts, patches_t, w1v, w2v, b1, b2, gain, cot,
     emb, gw1, gw2,
     send, recv, lsem, starts, ends, srcs,
     sc, cc, g, nrm, sp, cp, xf, sqx,
@@ -82,7 +82,7 @@
     pe, ps, pr, sb, bk,
     g2, a2, c2, s2a, s2b, d2, e2, t2,
     g1, a1, c1, s1a, s1b, d1, e1, t1,
-    i1, i2, k1, k2, b1s, pk,
+    i1, i2, k1, k2, b1s, pk, w2p, w1,
 ):
     r = lax.axis_index("dp")
     t = lax.axis_index("tensor")
@@ -156,6 +156,11 @@
         high = sq.astype(BF)
         low = (sq - high.astype(F32)).astype(BF)
         sqx[t, :, 128 * i : 128 * i + 128] = dot(pick_bf, high, NT) + dot(pick_bf, low, NT)
+    for i in range(2):
+        for e in range(2):
+            w2p[e, 80 * i : 80 * i + 80] = w2v[i, e]
+    wide = w1v[...].astype(F32)
+    w1[...] = jnp.concatenate([wide[:, p] for p in range(4)], axis=1).astype(BF)
     gains = jnp.concatenate([gain[...].astype(F32).reshape(1, 160)] * 4, axis=1)
     b1s[...] = jnp.broadcast_to(b1[...].astype(F32).reshape(1, 320), (128, 320)).T.reshape(2, 2, 80, 128)
 
@@ -809,8 +814,7 @@
 
 def on_device(patches, norm_gain, w_first, b_first, w_second, b_second, counts, cotangent):
     patches_t = patches.T
-    w1 = w_first.reshape(80, FEAT)
-    w2p = w_second.T.reshape(2, 2, 80, 128).transpose(1, 0, 2, 3).reshape(2, UNITS, 128)
+    w2v = w_second.T.reshape(2, 2, 80, 128)
     cot = cotangent.reshape(SLOTS, ROWS, OUTW)
 
     vmem = pl.BlockSpec(memory_space=pltpu.VMEM)
@@ -877,6 +881,8 @@
             V((2, UNITS, 128), BF),
             V((2, 2, 80, 128), F32),
             V((SLOTS, ROWS, FEAT), BF),
+            V((2, UNITS, 128), BF),
+            V((80, FEAT), BF),
         ],
         compiler_params=pltpu.CompilerParams(
             collective_id=0, has_side_effects=True, vmem_limit_bytes=56 * 1024 * 1024
@@ -884,7 +890,7 @@
         cost_estimate=pl.CostEstimate(
             flops=3_700_000_000, bytes_accessed=3_000_000, transcendentals=200_000
         ),
-    )(counts, patches_t, w1, w2p, b_first, b_second, norm_gain, cot)
+    )(counts, patches_t, w_first, w2v, b_first, b_second, norm_gain, cot)
     embeddings = emb.reshape(SLOTS * ROWS, OUTW)
     grad_w1 = gw1.reshape(80, 4, 160)
     grad_w2 = gw2.reshape(2, 2, 80, 128).transpose(3, 1, 0, 2).reshape(128, 320)

time: 122 us -> 119 us (0.975)
  local copies, waits for them, and re-layouts: 6.62 us -> 4.25 us
    reshape x2 -> x0, local copies, waits for them, and re-layouts: 2.36 us -> none  [the longest x1 1.56 us: on_device(): w_second.T.reshape(2, 2, 80, 128).transpose(1, 0, 2, 3)]
where the time goes in v4:
time: 119 us
  Pallas kernels  114 us (96%)
  local copies, waits for them, and re-layouts  4.25 us (4%)
    pallas_call x1, Pallas kernels, on_device(): pl.pallas_call(kernel, name='merger', out_shape=(jax.ShapeDtypeStruct((SL...  114 us

profile of v4, /device:TPU:164, one launch (start us, length us, event | category | flops | bytes accessed | tf_op | source)
XLA Modules:
  0.0 119.2 jit_solution(5356815254079111494)
XLA Ops:
  0.6 114.3 %merger.1 = (bf16[32,16,512]{2,1,0:T(8,128)(2,1)}, bf16[80,640]{1,0:T(8,128)(2,1)}, bf16[2,160,128]{2,1,0:T(8,128)(2,1)}) custom-call(s32[32]{0:T(128)} %counts.1, bf16[160,2048]{1,0:T(8,128)(2,1)} %bitcast.13, bf16[80,4,160]{2,1,0:T(4,128)(2,1)} %w1v.1, bf16[2,2,80,128]{3,2,1,0:T(8,128)(2,1)} %bitcast.15, bf16[320]{0:T(512)(128)(2,1)} %b1.1, ...), custom_call_target="tpu_custom_call" | custom-call | flops 3700000000 | bytes 3000000 | tf_op jit(solution)/shard_map/merger/pallas_call | solution.py:823
  114.9 0.0 copy-start
  114.9 1.6 %copy.11 = bf16[128,2,2,80]{0,3,2,1:T(8,128)(2,1)} copy(bf16[128,2,2,80]{0,3,1,2:T(8,128)(2,1)} %bitcast.12) | data formatting | bytes 163840 | tf_op jit(solution)/shard_map/transpose | solution.py:896
  116.5 0.0 copy-done
  116.5 0.8 reshape.27
  117.3 1.9 %copy.13 = bf16[512,512]{1,0:T(8,128)(2,1)} copy(bf16[512,512]{1,0:T(8,128)(2,1)} %bitcast.10) | data formatting | bytes 1048576
Async XLA Ops:
  114.9 1.6 %copy-start = (bf16[80,640]{1,0:T(8,128)(2,1)S(1)}, bf16[80,640]{1,0:T(8,128)(2,1)}, u32[]{:S(2)}) copy-start(bf16[80,640]{1,0:T(8,128)(2,1)} %get-tuple-element.7) | copy-start | bytes 307204

commit v5 on v4

--- a/solution.py
+++ b/solution.py
@@ -63,8 +63,8 @@
     def landed(self, dst, sem, dev):
         self.make(dst, dst, sem, dev).wait_recv()
 
-    def finish(self):
-        for item in self.open:
+    def finish(self, items):
+        for item in items:
             if callable(item):
                 item()
             else:
@@ -755,6 +755,8 @@
         return carry
 
     lax.fori_loop(0, CHIPS, pack_home, 0)
+    before = links.open
+    links.open = []
     home_base = links.take(CHIPS)
     exchange(sb, bk, home_base)
 
@@ -794,6 +796,7 @@
 
     links.open.append(lambda: back_plane(lambda copy: copy.wait_send()))
 
+    links.finish(before)
     exchanged(bk, home_base)
 
     def home(j, carry):
@@ -809,7 +812,7 @@
         links.landed(gw1, back1 + 1, plane(mid_chip))
         links.landed(gw2, back + 2, plane(mid_chip))
 
-    links.finish()
+    links.finish(links.open)
 
 
 def on_device(patches, norm_gain, w_first, b_first, w_second, b_second, counts, cotangent):

time: 119 us -> 119 us (level)
  no operation moved by 1% of the time
where the time goes in v5:
time: 119 us
  Pallas kernels  114 us (96%)
  local copies, waits for them, and re-layouts  4.25 us (4%)
    pallas_call x1, Pallas kernels, on_device(): pl.pallas_call(kernel, name='merger', out_shape=(jax.ShapeDtypeStruct((SL...  114 us

profile of v5, /device:TPU:164, one launch (start us, length us, event | category | flops | bytes accessed | tf_op | source)
XLA Modules:
  0.0 118.7 jit_solution(9452155073118241054)
XLA Ops:
  0.6 113.8 %merger.1 = (bf16[32,16,512]{2,1,0:T(8,128)(2,1)}, bf16[80,640]{1,0:T(8,128)(2,1)}, bf16[2,160,128]{2,1,0:T(8,128)(2,1)}) custom-call(s32[32]{0:T(128)} %counts.1, bf16[160,2048]{1,0:T(8,128)(2,1)} %bitcast.13, bf16[80,4,160]{2,1,0:T(4,128)(2,1)} %w1v.1, bf16[2,2,80,128]{3,2,1,0:T(8,128)(2,1)} %bitcast.15, bf16[320]{0:T(512)(128)(2,1)} %b1.1, ...), custom_call_target="tpu_custom_call" | custom-call | flops 3700000000 | bytes 3000000 | tf_op jit(solution)/shard_map/merger/pallas_call | solution.py:826
  114.4 0.0 copy-start
  114.4 1.6 %copy.11 = bf16[128,2,2,80]{0,3,2,1:T(8,128)(2,1)} copy(bf16[128,2,2,80]{0,3,1,2:T(8,128)(2,1)} %bitcast.12) | data formatting | bytes 163840 | tf_op jit(solution)/shard_map/transpose | solution.py:899
  116.0 0.0 copy-done
  116.0 0.8 reshape.27
  116.8 1.9 %copy.13 = bf16[512,512]{1,0:T(8,128)(2,1)} copy(bf16[512,512]{1,0:T(8,128)(2,1)} %bitcast.10) | data formatting | bytes 1048576
Async XLA Ops:
  114.4 1.6 %copy-start = (bf16[80,640]{1,0:T(8,128)(2,1)S(1)}, bf16[80,640]{1,0:T(8,128)(2,1)}, u32[]{:S(2)}) copy-start(bf16[80,640]{1,0:T(8,128)(2,1)} %get-tuple-element.7) | copy-start | bytes 307204

commit v6 on v5

--- a/solution.py
+++ b/solution.py
@@ -73,7 +73,7 @@
 
 def kernel(
     counts, patches_t, w1v, w2v, b1, b2, gain, cot,
-    emb, gw1, gw2,
+    emb, gw1v, gw2v,
     send, recv, lsem, starts, ends, srcs,
     sc, cc, g, nrm, sp, cp, xf, sqx,
     w1f, w2t,
@@ -82,7 +82,7 @@
     pe, ps, pr, sb, bk,
     g2, a2, c2, s2a, s2b, d2, e2, t2,
     g1, a1, c1, s1a, s1b, d1, e1, t1,
-    i1, i2, k1, k2, b1s, pk, w2p, w1,
+    i1, i2, k1, k2, b1s, pk, w2p, w1, gw1, gw2,
 ):
     r = lax.axis_index("dp")
     t = lax.axis_index("tensor")
@@ -812,6 +812,12 @@
         links.landed(gw1, back1 + 1, plane(mid_chip))
         links.landed(gw2, back + 2, plane(mid_chip))
 
+    for i in range(2):
+        for e in range(2):
+            gw2v[i, e] = gw2[e, 80 * i : 80 * i + 80]
+    wide = gw1[...].astype(F32)
+    parts = [wide[:, 160 * p : 160 * p + 160] for p in range(4)]
+    gw1v[...] = jnp.stack(parts, axis=1).astype(BF)
     links.finish(links.open)
 
 
@@ -828,8 +834,8 @@
         name="merger",
         out_shape=(
             jax.ShapeDtypeStruct((SLOTS, ROWS, OUTW), BF),
-            jax.ShapeDtypeStruct((80, FEAT), BF),
-            jax.ShapeDtypeStruct((2, UNITS, 128), BF),
+            jax.ShapeDtypeStruct((80, 4, 160), BF),
+            jax.ShapeDtypeStruct((2, 2, 80, 128), BF),
         ),
         in_specs=[pl.BlockSpec(memory_space=pltpu.SMEM)] + [vmem] * 7,
         out_specs=(vmem, vmem, vmem),
@@ -886,6 +892,8 @@
             V((SLOTS, ROWS, FEAT), BF),
             V((2, UNITS, 128), BF),
             V((80, FEAT), BF),
+            V((80, FEAT), BF),
+            V((2, UNITS, 128), BF),
         ],
         compiler_params=pltpu.CompilerParams(
             collective_id=0, has_side_effects=True, vmem_limit_bytes=56 * 1024 * 1024
@@ -895,9 +903,8 @@
         ),
     )(counts, patches_t, w_first, w2v, b_first, b_second, norm_gain, cot)
     embeddings = emb.reshape(SLOTS * ROWS, OUTW)
-    grad_w1 = gw1.reshape(80, 4, 160)
-    grad_w2 = gw2.reshape(2, 2, 80, 128).transpose(3, 1, 0, 2).reshape(128, 320)
-    return embeddings, grad_w1, grad_w2
+    grad_w2 = gw2.reshape(320, 128).T
+    return embeddings, gw1, grad_w2
 
 
 def solution(mesh):

time: 119 us -> 119 us (level)
    unnamed x3 -> x7, local copies, waits for them, and re-layouts: 1.87 us -> 3.48 us
    transpose x1 -> x0, local copies, waits for them, and re-layouts: 1.56 us -> none  [on_device(): grad_w2 = gw2.reshape(2, 2, 80, 128).transpose(3, 1, 0, 2).reshape(128, 320)]
where the time goes in v6:
time: 119 us; the launch traced here: 118 us
  Pallas kernels  114 us (96%)
  local copies, waits for them, and re-layouts  3.48 us (3%)
    pallas_call x1, Pallas kernels, on_device(): pl.pallas_call(kernel, name='merger', out_shape=(jax.ShapeDtypeStruct((SL...  114 us
    unnamed x7, local copies, waits for them, and re-layouts  3.48 us

profile of v6, /device:TPU:164, one launch (start us, length us, event | category | flops | bytes accessed | tf_op | source)
XLA Modules:
  0.0 118.4 jit_solution(13316865691394202285)
XLA Ops:
  0.6 114.3 %merger.1 = (bf16[32,16,512]{2,1,0:T(8,128)(2,1)}, bf16[80,4,160]{2,1,0:T(4,128)(2,1)}, bf16[2,2,80,128]{3,2,1,0:T(8,128)(2,1)}) custom-call(s32[32]{0:T(128)} %counts.1, bf16[160,2048]{1,0:T(8,128)(2,1)} %bitcast.11, bf16[80,4,160]{2,1,0:T(4,128)(2,1)} %w1v.1, bf16[2,2,80,128]{3,2,1,0:T(8,128)(2,1)} %bitcast.13, bf16[320]{0:T(512)(128)(2,1)} %b1.1, ...), custom_call_target="tpu_custom_call" | custom-call | flops 3700000000 | bytes 3000000 | tf_op jit(solution)/shard_map/merger/pallas_call | solution.py:832
  114.9 0.0 copy-start
  114.9 1.9 %copy.14 = bf16[512,512]{1,0:T(8,128)(2,1)} copy(bf16[512,512]{1,0:T(8,128)(2,1)} %bitcast.9) | data formatting | bytes 1048576
  116.8 0.0 copy-done
  116.8 0.0 copy-start.1
  116.8 0.7 copy.15
  117.5 0.3 copy-done.1
  117.8 0.6 copy.16
Async XLA Ops:
  114.9 1.9 %copy-start = (bf16[80,4,160]{2,1,0:T(4,128)(2,1)S(1)}, bf16[80,4,160]{2,1,0:T(4,128)(2,1)}, u32[]{:S(2)}) copy-start(bf16[80,4,160]{2,1,0:T(4,128)(2,1)} %get-tuple-element.13) | copy-start | bytes 307204
  116.8 0.9 copy-start.1
